TPU v7x, 32 devices: a whole 2x2x4 slice. The times are simulated.
32 devices in a mesh: cand: 8 (over z, y), tp: 4 (over x, core).
Axes of the slice: x: 2, y: 2, z: 4, core: 2. Of those that a mesh axis runs over, the one named last changes fastest.
Arguments:
- reward_query: bfloat16 [64, 32, 8192], P('cand', None, 'tp'), may hold values from -170 to 170
- reward_new: bfloat16 [64, 2, 32, 1024], P('cand', None, None, 'tp'), may hold values from -7 to 7
- reward_key_value_cache: bfloat16 [64, 2, 768, 1024], P('cand', None, None, 'tp'), may hold values from -6 to 6
- reward_length: int32 [64], P('cand'), may hold values from 1 to 768
- out_weight: bfloat16 [8192, 4096], P('tp'), may hold values from -0.09375 to 0.09375
- policy_cache: bfloat16 [64, 2, 768, 1024], P('cand', None, None, 'tp'), may hold values from -6 to 6
- policy_length: int32 [64], replicated, may hold values from 1 to 767
- source: int32 [32], replicated, may hold values from 0 to 63, as said below
- policy_query: bfloat16 [32, 8192], P('cand', 'tp'), may hold values from -170 to 170
- policy_new: bfloat16 [32, 2, 1024], P('cand', None, 'tp'), may hold values from -7 to 7
Outputs:
- reward_out: bfloat16 [2048, 4096], P('cand', 'tp')
- compacted: bfloat16 [32, 2, 768, 1024], P('cand', None, None, 'tp')
- policy_attn: bfloat16 [32, 8192], P('cand', 'tp')
Inputs may be any that keep to these rules, and one draw needn't show every extreme that they name: `source`: distinct candidate indices; the 8 candidates of each index of cand are named exactly 4 times.
All inputs are finite; a program needn't handle non-finite values.
Results may differ from a plain program's by a relative error of at most 0.0057.
Values may be sent and summed in bfloat16 or wider, within the bound.
No kernel may reach another device: no remote copies, remote signals or barrier semaphores. Data moves between devices by JAX's collectives and lax.ppermute only.
A program may use at most 128 MiB of HBM per device.

v0:
```python
import functools

import jax
import jax.numpy as jnp
from jax import lax
from jax.experimental import pallas as pl
from jax.experimental.pallas import tpu as pltpu
from jax.sharding import PartitionSpec as P

ASKING_UNITS = 64
SHARED_KV_UNITS = 8
ATTN_DIM = 128
NEW_TOKEN_COUNT = 32
CACHE_LENGTH = 768

GRID_Z = 4
GRID_Y = 2
GRID = GRID_Z * GRID_Y
ROUNDS = [(2, 1)] + [(1, 2)] * 8
LAST = len(ROUNDS) - 1
PLACE = [3 * sum(many for many, _ in ROUNDS[:turn]) for turn in range(len(ROUNDS) + 1)]
SENT = PLACE[-1]
NEXT = 2 * SENT
LOG = 128
SLOTS = 4 * GRID
UP = [(n, n + 2) for n in range(6)]
DOWN = [(n + 2, n) for n in range(6)]
ACROSS = [(n, n + 1 - 2 * (n % 2)) for n in range(8)]

VMEM_GRANT = 60 * 1024 * 1024
LOG2_E = 1.4426950408889634

ANY = pl.BlockSpec(memory_space=pl.ANY)
HBM = pl.BlockSpec(memory_space=pltpu.HBM)
SMEM = pl.BlockSpec(memory_space=pltpu.SMEM)
VMEM = pl.BlockSpec(memory_space=pltpu.VMEM)
LITTLE = pl.CostEstimate(flops=1000, bytes_accessed=1000, transcendentals=0)


def choose(state, many, lag, open_all=False):
    z, y, wait, last_z, last_y, lane_y = state
    me = lax.axis_index("cand")
    need_z = z != last_z
    next_y = jnp.where(need_z, lane_y, last_y)
    move_y = y != next_y
    move = jnp.where(move_y, 2, jnp.where(need_z, jnp.where(last_z > z, 0, 1), 3))
    after = jnp.where(need_z & (lane_y != last_y), 1, 0)
    steps = jnp.abs(z - last_z) + jnp.where(move_y, 1, 0) + after
    left = jnp.sum(jnp.where(move < 3, 1.0, 0.0)).astype(jnp.int32)
    ready = move < 3
    if not open_all:
        ready = ready & (wait <= 0)
    link = jnp.where(ready, move * GRID + z * GRID_Y + y, 99)
    column = lax.broadcasted_iota(jnp.int32, (1, 128), 1)
    key = (steps * 128 + 127 - column).astype(jnp.float32)
    rows = lax.broadcasted_iota(jnp.int32, (3 * GRID, 128), 0)
    names = (lax.broadcasted_iota(jnp.int32, (3 * GRID, 128), 1) + 1).astype(jnp.float32)
    keys = jnp.where(rows == link, key, -1.0)
    partner = me + 1 - 2 * lax.rem(me, 2)
    out_scale = (
        jnp.where(rows == me, 1.0, 0.0)
        + jnp.where(rows == me + GRID, 128.0, 0.0)
        + jnp.where(rows == me + 2 * GRID, 16384.0, 0.0)
    )
    in_scale = (
        jnp.where(rows == me - 2, 1.0, 0.0)
        + jnp.where((rows == me + 2 + GRID) & (rows < 2 * GRID), 128.0, 0.0)
        + jnp.where(rows == partner + 2 * GRID, 16384.0, 0.0)
    )
    moved = jnp.zeros_like(key)
    sent, got = [], []
    for _ in range(many):
        best = jnp.max(keys, axis=1, keepdims=True)
        won = (keys == best) & (keys >= 0.0)
        number = jnp.where(won, names, 0.0)
        keys = jnp.where(won, -1.0, keys)
        moved = jnp.maximum(moved, jnp.max(number, axis=0, keepdims=True))
        for packed, into in ((jnp.sum(number * out_scale), sent), (jnp.sum(number * in_scale), got)):
            packed = packed.astype(jnp.int32)
            into += [packed & 127, (packed >> 7) & 127, packed >> 14]
    moved = moved > 0.0
    z = jnp.where(moved, z + jnp.where(move == 0, 1, 0) - jnp.where(move == 1, 1, 0), z)
    y = jnp.where(moved & (move == 2), 1 - y, y)
    wait = jnp.where(moved, lag - 1, jnp.maximum(wait - 1, 0))
    return [z, y, wait, last_z, last_y, lane_y], sent, got, left


def parcel_from(number, source_ref, log_ref, cache_ref, arrivals, held_ref, target, sem):
    index = number - 1
    slot, half = index >> 1, index & 1
    per_index = cache_ref.shape[0]
    local = source_ref[jnp.maximum(slot, 0)] - lax.axis_index("cand") * per_index
    own = (number > 0) & (local >= 0) & (local < per_index)
    elsewhere = (number > 0) & jnp.logical_not(own)

    @pl.when(own)
    def _():
        pltpu.make_async_copy(cache_ref.at[local, half], target, sem).start()

    for i, ref in enumerate(arrivals):
        match = elsewhere & (log_ref[i] == number)
        if held_ref is not None:
            elsewhere = elsewhere & (log_ref[i] != number)

        @pl.when(match)
        def _(ref=ref):
            pltpu.make_async_copy(ref, target, sem).start()

    if held_ref is not None:

        @pl.when(elsewhere)
        def _():
            pltpu.make_async_copy(held_ref.at[index], target, sem).start()


def each_parcel(arrivals):
    parcels = []
    for first in range(0, len(arrivals), 3):
        triple = arrivals[first : first + 3]
        parcels += [ref.at[i] for i in range(triple[0].shape[0]) for ref in triple]
    return parcels


def lay_out(numbers, source_ref, log_ref, cache_ref, arrivals, sends, room, in_sem, out_sem):
    many = sends[0].shape[0]

    def put(i):
        return pltpu.make_async_copy(room.at[i], sends[i % 3].at[i // 3], out_sem.at[i])

    def begin():
        for i in range(3 * many):
            parcel_from(numbers[i], source_ref, log_ref, cache_ref, arrivals, None, room.at[i], in_sem.at[i])

    def end():
        for i in range(3 * many):

            @pl.when(numbers[i] > 0)
            def _(i=i):
                pltpu.make_async_copy(cache_ref.at[0, 0], room.at[i], in_sem.at[i]).wait()
                put(i).start()

        for i in range(3 * many):

            @pl.when(numbers[i] > 0)
            def _(i=i):
                put(i).wait()

    return begin, end


def lay_out_scratch(many, cache):
    return [
        pltpu.VMEM((3 * many,) + cache.shape[2:], cache.dtype),
        pltpu.SemaphoreType.DMA((3 * many,)),
        pltpu.SemaphoreType.DMA((3 * many,)),
    ]


def sends_of(many, cache):
    return [jax.ShapeDtypeStruct((many,) + cache.shape[2:], cache.dtype)] * 3


def first_kernel(source_ref, cache_ref, log_out, state_out, up, down, across, *scratch):
    parcel = lax.broadcasted_iota(jnp.int32, (1, 128), 1)
    owner = jnp.zeros_like(parcel)
    for i in range(SLOTS):
        owner = jnp.where((parcel >> 1) == i, source_ref[i] >> 3, owner)
    target = jnp.where(parcel < 2 * SLOTS, parcel >> 3, 0)
    state = [owner >> 1, owner & 1, jnp.zeros_like(parcel), target >> 1, target & 1, parcel & 1]
    state, sent, got, _ = choose(state, *ROUNDS[0])
    begin, end = lay_out(sent, source_ref, None, cache_ref, [], (up, down, across), *scratch)
    begin()
    for i in range(LOG):
        log_out[i] = 0
    for i in range(len(got)):
        log_out[i] = got[i]
        log_out[SENT + i] = sent[i]
    for i in range(6):
        state_out[i : i + 1, :] = state[i]
    end()


def first_stage(source, cache):
    many, _ = ROUNDS[0]
    log, state, *sends = pl.pallas_call(
        first_kernel,
        out_shape=[jax.ShapeDtypeStruct((LOG,), jnp.int32), jax.ShapeDtypeStruct((8, 128), jnp.int32)]
        + sends_of(many, cache),
        in_specs=[SMEM, HBM],
        out_specs=[SMEM, VMEM, HBM, HBM, HBM],
        scratch_shapes=lay_out_scratch(many, cache),
        compiler_params=pltpu.CompilerParams(vmem_limit_bytes=VMEM_GRANT),
        cost_estimate=LITTLE,
    )(source, cache)
    return log, state, sends


def plan_kernel(log_ref, state_ref, log_out, state_out, left_out):
    state = [state_ref[i : i + 1, :] for i in range(6)]
    for i in range(LOG):
        log_out[i] = log_ref[i]
    for turn in range(1, len(ROUNDS)):
        state, sent, got, _ = choose(state, *ROUNDS[turn])
        for i in range(len(got)):
            log_out[PLACE[turn] + i] = got[i]
            log_out[SENT + PLACE[turn] + i] = sent[i]
    state, sent, got, left = choose(state, 1, 1, True)
    for i in range(3):
        log_out[NEXT + i] = sent[i]
        log_out[NEXT + 3 + i] = got[i]
    left_out[0] = left
    for i in range(6):
        state_out[i : i + 1, :] = state[i]


def plan(log, state):
    return pl.pallas_call(
        plan_kernel,
        out_shape=[
            jax.ShapeDtypeStruct(log.shape, jnp.int32),
            jax.ShapeDtypeStruct(state.shape, jnp.int32),
            jax.ShapeDtypeStruct((1,), jnp.int32),
        ],
        in_specs=[SMEM, VMEM],
        out_specs=[SMEM, VMEM, SMEM],
        cost_estimate=LITTLE,
    )(log, state)


def stage_kernel(turn, count, source_ref, log_ref, cache_ref, *refs):
    arrivals = each_parcel(refs[:count])
    sends = refs[count : count + 3]
    many, _ = ROUNDS[turn]
    sent = [log_ref[SENT + PLACE[turn] + i] for i in range(3 * many)]
    begin, end = lay_out(sent, source_ref, log_ref, cache_ref, arrivals, sends, *refs[count + 3 :])
    begin()
    end()


def stage(source, log, cache, arrivals, turn):
    many, _ = ROUNDS[turn]
    return pl.pallas_call(
        functools.partial(stage_kernel, turn, len(arrivals)),
        out_shape=sends_of(many, cache),
        in_specs=[SMEM, SMEM, HBM] + [ANY] * len(arrivals),
        out_specs=[HBM] * 3,
        scratch_shapes=lay_out_scratch(many, cache),
        compiler_params=pltpu.CompilerParams(vmem_limit_bytes=VMEM_GRANT),
        cost_estimate=LITTLE,
    )(source, log, cache, *arrivals)


def late_kernel(count, source_ref, log_ref, state_ref, cache_ref, *refs):
    arrivals = each_parcel(refs[:count])
    held_in, log_out, state_out, left_out, up, down, across, held_out, store_sem, send_sem = refs[count:]
    sends = (up, down, across)
    latest = arrivals[-3:]
    place = PLACE[LAST]
    number = [log_ref[place + i] for i in range(3)]
    for i, ref in enumerate(latest):

        @pl.when(number[i] > 0)
        def _(i=i, ref=ref):
            pltpu.make_async_copy(ref, held_out.at[number[i] - 1], store_sem.at[i]).start()

    sent = [log_ref[NEXT + i] for i in range(3)]
    for i in range(3):
        parcel_from(
            sent[i], source_ref, log_ref, cache_ref, arrivals, held_in, sends[i].at[0], send_sem.at[i]
        )
    state, next_sent, next_got, left = choose([state_ref[i : i + 1, :] for i in range(6)], 1, 1, True)
    for i in range(place):
        log_out[i] = log_ref[i]
    for i in range(3):
        log_out[place + i] = log_ref[NEXT + 3 + i]
        log_out[NEXT + i] = next_sent[i]
        log_out[NEXT + 3 + i] = next_got[i]
    left_out[0] = left
    for i in range(6):
        state_out[i : i + 1, :] = state[i]
    for i in range(3):

        @pl.when(sent[i] > 0)
        def _(i=i):
            pltpu.make_async_copy(cache_ref.at[0, 0], sends[i].at[0], send_sem.at[i]).wait()

    for i, ref in enumerate(latest):

        @pl.when(number[i] > 0)
        def _(i=i, ref=ref):
            pltpu.make_async_copy(ref, held_out.at[number[i] - 1], store_sem.at[i]).wait()


def late_stage(source, log, state, cache, arrivals, held):
    count = len(arrivals)
    out = pl.pallas_call(
        functools.partial(late_kernel, count),
        out_shape=[
            jax.ShapeDtypeStruct((LOG,), jnp.int32),
            jax.ShapeDtypeStruct((8, 128), jnp.int32),
            jax.ShapeDtypeStruct((1,), jnp.int32),
        ]
        + sends_of(1, cache)
        + [jax.ShapeDtypeStruct(held.shape, held.dtype)],
        in_specs=[SMEM, SMEM, VMEM, HBM] + [ANY] * (count - 3) + [VMEM] * 3 + [HBM],
        out_specs=[SMEM, VMEM, SMEM, VMEM, VMEM, VMEM, HBM],
        scratch_shapes=[pltpu.SemaphoreType.DMA((3,)), pltpu.SemaphoreType.DMA((3,))],
        input_output_aliases={4 + count: 6},
        cost_estimate=LITTLE,
    )(source, log, state, cache, *arrivals, held)
    log, state, left, *rest = out
    return log, state, left, rest[:3], rest[3]


def room_kernel(out_ref):
    pass


def room(parcels, cache):
    return pl.pallas_call(
        room_kernel,
        out_shape=jax.ShapeDtypeStruct((parcels,) + cache.shape[2:], cache.dtype),
        out_specs=HBM,
        cost_estimate=LITTLE,
    )()


def exchange(sends):
    up, down, across = sends
    return (
        lax.ppermute(up, "cand", UP),
        lax.ppermute(down, "cand", DOWN),
        lax.ppermute(across, "cand", ACROSS),
    )


def slot_attention(q_rows, keys, values, length, score_scale):
    scores = lax.dot_general(q_rows, keys, (((1,), (1,)), ((), ())), preferred_element_type=jnp.float32)
    scores = scores * score_scale
    position = lax.broadcasted_iota(jnp.int32, scores.shape, 1)
    scores = jnp.where(position <= length, scores, -1e30)
    weights = jnp.exp(scores - jnp.max(scores, axis=1, keepdims=True))
    total = jnp.sum(weights, axis=1, keepdims=True)
    mixed = jnp.dot(weights.astype(jnp.bfloat16), values, preferred_element_type=jnp.float32)
    return mixed / total


def finish_kernel(count, *refs):
    source_ref, length_ref, log_ref, query_ref, new_ref, cache_ref = refs[:6]
    arrivals = each_parcel(refs[6 : 6 + count])
    held_ref, compacted_ref, attn_ref, rows, attn, sem, out_sem = refs[6 + count :]
    me = lax.axis_index("cand")
    slots, _, depth, width = rows.shape
    kv_heads = width // ATTN_DIM
    group = query_ref.shape[1] // width
    for s in range(slots):
        for half in range(2):
            number = (me * slots + s) * 2 + half + 1
            parcel_from(
                number, source_ref, log_ref, cache_ref, arrivals, held_ref, rows.at[s, half], sem.at[2 * s + half]
            )
    query = query_ref[...].astype(jnp.float32)
    for s in range(slots):
        length = length_ref[source_ref[me * slots + s]]
        base = pl.multiple_of((length >> 4) << 4, 16)
        for half in range(2):
            pltpu.make_async_copy(cache_ref.at[0, 0], rows.at[s, half], sem.at[2 * s + half]).wait()
            window = rows[s, half, pl.ds(base, 16), :]
            row = lax.broadcasted_iota(jnp.int32, window.shape, 0)
            fresh_row = new_ref[s, half : half + 1, :]
            rows[s, half, pl.ds(base, 16), :] = jnp.where(
                row == length - base, fresh_row.astype(jnp.float32), window.astype(jnp.float32)
            ).astype(window.dtype)
            pltpu.make_async_copy(rows.at[s, half], compacted_ref.at[s, half], out_sem.at[2 * s + half]).start()
        for k in range(kv_heads):
            columns = slice(k * ATTN_DIM, (k + 1) * ATTN_DIM)
            heads = [slice((k * group + g) * ATTN_DIM, (k * group + g + 1) * ATTN_DIM) for g in range(group)]
            mixed = slot_attention(
                jnp.concatenate([query[s : s + 1, h] for h in heads], axis=0).astype(query_ref.dtype),
                rows[s, 0, :, columns],
                rows[s, 1, :, columns],
                length,
                ATTN_DIM ** (-0.5),
            )
            for g, h in enumerate(heads):
                attn[s : s + 1, h] = mixed[g : g + 1, :]
    attn_ref[...] = attn[...].astype(attn_ref.dtype)
    for s in range(slots):
        for half in range(2):
            pltpu.make_async_copy(rows.at[s, half], compacted_ref.at[s, half], out_sem.at[2 * s + half]).wait()


def finish(source, policy_length, log, query, new, cache, arrivals, held):
    slots = query.shape[0]
    _, _, depth, width = cache.shape
    return pl.pallas_call(
        functools.partial(finish_kernel, len(arrivals)),
        out_shape=[
            jax.ShapeDtypeStruct((slots, 2, depth, width), cache.dtype),
            jax.ShapeDtypeStruct(query.shape, query.dtype),
        ],
        in_specs=[SMEM, SMEM, SMEM, VMEM, VMEM, HBM] + [ANY] * len(arrivals) + [HBM],
        out_specs=[HBM, VMEM],
        scratch_shapes=[
            pltpu.VMEM((slots, 2, depth, width), cache.dtype),
            pltpu.VMEM(query.shape, jnp.float32),
            pltpu.SemaphoreType.DMA((2 * slots,)),
            pltpu.SemaphoreType.DMA((2 * slots,)),
        ],
        compiler_params=pltpu.CompilerParams(vmem_limit_bytes=VMEM_GRANT),
        cost_estimate=LITTLE,
    )(source, policy_length, log, query, new, cache, *arrivals, held)


def routed_policy(policy_cache, policy_length, source, policy_query, policy_new, reward_inputs):
    first_log, first_state, sends = first_stage(source, policy_cache)
    arrivals = list(exchange(sends))
    log, state, left = plan(first_log, first_state)
    log, *reward_inputs = lax.optimization_barrier((log, *reward_inputs))
    give, keep = reward_share(*reward_inputs, by_core=True)
    log, give, keep = lax.optimization_barrier((log, give, keep))
    for turn in range(1, len(ROUNDS)):
        at_hand = arrivals[: 3 * sum(sent + lag <= turn for sent, (_, lag) in enumerate(ROUNDS[:turn]))]
        sends = stage(source, log, policy_cache, at_hand, turn)
        log, *sends = lax.optimization_barrier((log, *sends))
        arrivals += exchange(sends)
        if turn == 1:
            log, give = lax.optimization_barrier((log, give))
            give = lax.ppermute(give, "tp", [(0, 1), (1, 0), (2, 3), (3, 2)])
        if turn == 3:
            log, keep, give = lax.optimization_barrier((log, keep, give))
            mine, other = add_cores(keep, give)
            log, mine, other = lax.optimization_barrier((log, mine, other))
            other = lax.ppermute(other, "tp", [(0, 2), (2, 0), (1, 3), (3, 1)])
    early, latest = arrivals[:-3], arrivals[-3:]
    reward_out = (mine + other.astype(jnp.float32)).astype(jnp.bfloat16)
    left, reward_out = lax.optimization_barrier((left, reward_out))

    def unfinished(carry):
        return carry[0][0] > 0

    def one_round(carry):
        _, log, state, latest, held = carry
        log, state, left, sends, held = late_stage(source, log, state, policy_cache, early + latest, held)
        return left, log, state, list(exchange(sends)), held

    held = room(2 * SLOTS, policy_cache)
    _, log, _, latest, held = lax.while_loop(unfinished, one_round, (left, log, state, latest, held))
    compacted, attn = finish(
        source, policy_length, log, policy_query, policy_new, policy_cache, early + latest, held
    )
    return reward_out, compacted, attn


def spread_policy(policy_cache, policy_length, source, policy_query, policy_new, reward_inputs):
    reward_out = add_shares(reward_share(*reward_inputs)[0])
    attention_clusters = ASKING_UNITS // SHARED_KV_UNITS
    score_scale = ATTN_DIM ** (-0.5)
    kv_heads = policy_cache.shape[-1] // ATTN_DIM
    cache_rows = lax.iota(jnp.int32, CACHE_LENGTH)
    slot_count = policy_query.shape[0]
    per_index = policy_cache.shape[0]
    owner = source // per_index
    slots = lax.iota(jnp.int32, source.shape[0])
    earlier = (owner[:, None] == owner[None, :]) & (slots[None, :] < slots[:, None])
    rank = jnp.sum(earlier.astype(jnp.int32), axis=1)
    me = lax.axis_index("cand")
    lane = lax.iota(jnp.int32, slot_count)
    mine = (owner[None, :] == me) & (rank[None, :] == lane[:, None])
    named = jnp.sum(jnp.where(mine, source[None, :] - me * per_index, 0), axis=1)
    picked = jnp.take(policy_cache, named, axis=0)
    spread = lax.all_to_all(picked, "cand", split_axis=2, concat_axis=0, tiled=True)
    selected = jnp.take(spread, owner * slot_count + rank, axis=0)
    moved = lax.all_to_all(selected, "cand", split_axis=0, concat_axis=2, tiled=True)
    local_source = lax.dynamic_slice_in_dim(source, lax.axis_index("cand") * slot_count, slot_count)
    slot_lengths = jnp.take(policy_length, local_source)
    compacted = jnp.where(
        cache_rows[None, None, :, None] == slot_lengths[:, None, None, None],
        policy_new[:, :, None, :],
        moved,
    )
    slot_heads = policy_query.reshape(slot_count, kv_heads, attention_clusters, ATTN_DIM)
    slot_keys = compacted[:, 0].reshape(slot_count, CACHE_LENGTH, kv_heads, ATTN_DIM)
    slot_values = compacted[:, 1].reshape(slot_count, CACHE_LENGTH, kv_heads, ATTN_DIM)
    slot_scores = (
        jnp.einsum("skgd,spkd->skgp", slot_heads, slot_keys, preferred_element_type=jnp.float32)
        * score_scale
    )
    slot_visible = cache_rows[None, :] <= slot_lengths[:, None]
    slot_scores = jnp.where(slot_visible[:, None, None, :], slot_scores, -1e30)
    slot_weights = jax.nn.softmax(slot_scores, axis=-1).astype(jnp.bfloat16)
    policy_attn = jnp.einsum(
        "skgp,spkd->skgd", slot_weights, slot_values, preferred_element_type=jnp.float32
    )
    policy_attn = policy_attn.reshape(slot_count, kv_heads * attention_clusters * ATTN_DIM).astype(
        jnp.bfloat16
    )
    return reward_out, compacted, policy_attn


def reward_kernel(length_ref, query_ref, new_ref, cache_ref, weight_ref, *refs):
    out_refs = refs[:-9]
    query, new, cache, weight, rows, out, sem, weight_sem, out_sem = refs[-9:]
    candidates, tokens, units = query.shape
    depth, width = cache.shape[2:]
    kv_heads = width // ATTN_DIM
    group = units // width
    blocks, _, block = weight.shape
    scale = ATTN_DIM ** (-0.5) * LOG2_E
    token = lax.rem(lax.broadcasted_iota(jnp.int32, (group * tokens, tokens), 0), tokens)
    new_visible = lax.broadcasted_iota(jnp.int32, (group * tokens, tokens), 1) <= token
    by_rows = (((1,), (1,)), ((), ()))

    def inputs(i):
        return [
            pltpu.make_async_copy(query_ref.at[i], query.at[i], sem.at[4 * i]),
            pltpu.make_async_copy(cache_ref.at[i, 0], cache.at[i, 0], sem.at[4 * i + 1]),
            pltpu.make_async_copy(new_ref.at[i], new.at[i], sem.at[4 * i + 2]),
            pltpu.make_async_copy(cache_ref.at[i, 1], cache.at[i, 1], sem.at[4 * i + 3]),
        ]

    def fetch(j):
        first = j * block
        if len(out_refs) == 2:
            part, piece = divmod(j, blocks // 4)
            core = lax.rem(lax.axis_index("tp"), 2)
            core = 1 - core if part < 2 else core
            first = pl.multiple_of((core + 2 * (part % 2)) * (weight_ref.shape[1] // 4) + piece * block, block)
        return pltpu.make_async_copy(weight_ref.at[:, pl.ds(first, block)], weight.at[j], weight_sem.at[j])

    def put(j):
        target = out_refs[0].at[:, pl.ds(j * block, block)] if len(out_refs) == 1 else None
        if target is None:
            part, piece = divmod(j, blocks // 4)
            target = out_refs[part // 2].at[part % 2, :, pl.ds(piece * block, block)]
        return pltpu.make_async_copy(out.at[j % 2], target, out_sem.at[j % 2])

    for i in range(min(3, candidates)):
        for copy in inputs(i):
            copy.start()
    fetched = 0
    for i in range(candidates):
        for copy in inputs(i):
            copy.wait()
        if i + 3 < candidates:
            for copy in inputs(i + 3):
                copy.start()
        while fetched < blocks * (i + 1) // candidates:
            fetch(fetched).start()
            fetched += 1
        visible = lax.broadcasted_iota(jnp.int32, (1, depth), 1) < length_ref[i]
        for k in range(kv_heads):
            columns = slice(k * ATTN_DIM, (k + 1) * ATTN_DIM)
            heads = [slice((k * group + g) * ATTN_DIM, (k * group + g + 1) * ATTN_DIM) for g in range(group)]
            asked = jnp.concatenate([query[i, :, h] for h in heads], axis=0)
            old = lax.dot_general(asked, cache[i, 0, :, columns], by_rows, preferred_element_type=jnp.float32)
            fresh = lax.dot_general(asked, new[i, 0, :, columns], by_rows, preferred_element_type=jnp.float32)
            old = jnp.where(visible, old, -1e30)
            fresh = jnp.where(new_visible, fresh, -1e30)
            peak = jnp.maximum(jnp.max(old, axis=1, keepdims=True), jnp.max(fresh, axis=1, keepdims=True))
            old = jnp.exp2((old - peak) * scale)
            fresh = jnp.exp2((fresh - peak) * scale)
            total = jnp.sum(old, axis=1, keepdims=True) + jnp.sum(fresh, axis=1, keepdims=True)
            mixed = jnp.dot(old.astype(jnp.bfloat16), cache[i, 1, :, columns], preferred_element_type=jnp.float32)
            mixed += jnp.dot(fresh.astype(jnp.bfloat16), new[i, 1, :, columns], preferred_element_type=jnp.float32)
            mixed = (mixed / total).astype(rows.dtype)
            for g, h in enumerate(heads):
                rows[i * tokens : (i + 1) * tokens, h] = mixed[g * tokens : (g + 1) * tokens, :]
    for j in range(blocks):
        fetch(j).wait()
        if j >= 2:
            put(j - 2).wait()
        out[j % 2] = jnp.dot(rows[...], weight[j], preferred_element_type=jnp.float32)
        put(j).start()
    put(blocks - 2).wait()
    put(blocks - 1).wait()


def reward_share(query, new, cache, length, weight, by_core=False):
    candidates, tokens, units = query.shape
    features = weight.shape[1]
    block = 512
    shape = (2, candidates * tokens, features // 4) if by_core else (candidates * tokens, features)
    outputs = 2 if by_core else 1
    return pl.pallas_call(
        reward_kernel,
        out_shape=[jax.ShapeDtypeStruct(shape, jnp.float32)] * outputs,
        in_specs=[SMEM, HBM, HBM, HBM, HBM],
        out_specs=[HBM] * outputs,
        scratch_shapes=[
            pltpu.VMEM(query.shape, query.dtype),
            pltpu.VMEM(new.shape, new.dtype),
            pltpu.VMEM(cache.shape, cache.dtype),
            pltpu.VMEM((features // block, units, block), weight.dtype),
            pltpu.VMEM((candidates * tokens, units), query.dtype),
            pltpu.VMEM((2, candidates * tokens, block), jnp.float32),
            pltpu.SemaphoreType.DMA((4 * candidates,)),
            pltpu.SemaphoreType.DMA((features // block,)),
            pltpu.SemaphoreType.DMA((2,)),
        ],
        compiler_params=pltpu.CompilerParams(vmem_limit_bytes=VMEM_GRANT),
        cost_estimate=LITTLE,
    )(length, query, new, cache, weight)


def add_cores_kernel(keep_ref, got_ref, mine_ref, other_ref, keep, got, out, sem, out_sem):
    x = lax.axis_index("tp") // 2
    for i, part in enumerate((1 - x, x)):
        pltpu.make_async_copy(keep_ref.at[part], keep.at[i], sem.at[2 * i]).start()
        pltpu.make_async_copy(got_ref.at[part], got.at[i], sem.at[2 * i + 1]).start()
    for i, part in enumerate((1 - x, x)):
        pltpu.make_async_copy(keep_ref.at[part], keep.at[i], sem.at[2 * i]).wait()
        pltpu.make_async_copy(got_ref.at[part], got.at[i], sem.at[2 * i + 1]).wait()
        if i == 0:
            out[...] = (keep[i] + got[i]).astype(out.dtype)
            pltpu.make_async_copy(out, other_ref, out_sem.at[0]).start()
        else:
            keep[i] += got[i]
            pltpu.make_async_copy(keep.at[i], mine_ref, out_sem.at[1]).start()
    pltpu.make_async_copy(out, other_ref, out_sem.at[0]).wait()
    pltpu.make_async_copy(keep.at[1], mine_ref, out_sem.at[1]).wait()


def add_cores(keep, got):
    part = keep.shape[1:]
    return pl.pallas_call(
        add_cores_kernel,
        out_shape=[jax.ShapeDtypeStruct(part, jnp.float32), jax.ShapeDtypeStruct(part, jnp.bfloat16)],
        in_specs=[HBM, HBM],
        out_specs=[HBM, HBM],
        scratch_shapes=[
            pltpu.VMEM(keep.shape, jnp.float32),
            pltpu.VMEM(keep.shape, jnp.float32),
            pltpu.VMEM(part, jnp.bfloat16),
            pltpu.SemaphoreType.DMA((4,)),
            pltpu.SemaphoreType.DMA((2,)),
        ],
        compiler_params=pltpu.CompilerParams(vmem_limit_bytes=VMEM_GRANT),
        cost_estimate=LITTLE,
    )(keep, got)


def add_shares(share):
    return lax.psum_scatter(share, "tp", scatter_dimension=1, tiled=True).astype(jnp.bfloat16)


def body(
    cand_count,
    tp_count,
    reward_query,
    reward_new,
    reward_key_value_cache,
    reward_length,
    out_weight,
    policy_cache,
    policy_length,
    source,
    policy_query,
    policy_new,
):
    policy = spread_policy
    if (cand_count, tp_count, policy_cache.shape[0], source.shape[0]) == (GRID, 4, 8, SLOTS):
        policy = routed_policy
    reward_inputs = (reward_query, reward_new, reward_key_value_cache, reward_length, out_weight)
    return policy(policy_cache, policy_length, source, policy_query, policy_new, reward_inputs)


def solution(mesh):
    in_specs = (
        P("cand", None, "tp"),
        P("cand", None, None, "tp"),
        P("cand", None, None, "tp"),
        P("cand"),
        P("tp", None),
        P("cand", None, None, "tp"),
        P(),
        P(),
        P("cand", "tp"),
        P("cand", None, "tp"),
    )
    out_specs = (P("cand", "tp"), P("cand", None, None, "tp"), P("cand", "tp"))
    return jax.shard_map(
        functools.partial(body, mesh.shape["cand"], mesh.shape["tp"]),
        mesh=mesh,
        in_specs=in_specs,
        out_specs=out_specs,
        check_vma=False,
    )
```

profile of v0, /device:TPU:0, one launch (start us, length us, event | category | flops | bytes accessed | tf_op | source)
XLA Modules:
  0.0 153.1 jit_solution(17382483440580463677)
XLA Ops:
  0.6 3.9 %shard_map.121 = (s32[128]{0:T(128)}, s32[8,128]{1,0:T(8,128)}, bf16[2,768,256]{2,1,0:T(8,128)(2,1)}, bf16[2,768,256]{2,1,0:T(8,128)(2,1)}, bf16[2,768,256]{2,1,0:T(8,128)(2,1)}) custom-call(s32[32]{0:T(128)} %refs_0_.1, bf16[8,2,768,256]{3,2,1,0:T(8,128)(2,1)} %refs_5_.1), custom_call_target="tpu_custom_call" | custom-call | flops 1000 | bytes 1000 | tf_op jit(solution)/shard_map/pallas_call | solution.py:185
  4.6 5.0 %collective-permute-start.3 = (bf16[2,768,256]{2,1,0:T(8,128)(2,1)}, bf16[2,768,256]{2,1,0:T(8,128)(2,1)S(1)}, u32[]{:S(2)}, u32[]{:S(2)}) collective-permute-start(bf16[2,768,256]{2,1,0:T(8,128)(2,1)} %get-tuple-element.282), channel_id=1, source_target_pairs={{0,8},{4,12},{8,16},{12,20},{16,24},{20,28},{1,9},{5,13},{9,17},{1... | collective-permute-start | bytes 2359304 | tf_op jit(solution)/shard_map/ppermute | solution.py:331
  9.5 1.3 collective-permute-start.4
  10.8 1.6 %collective-permute-start.5 = (bf16[2,768,256]{2,1,0:T(8,128)(2,1)}, bf16[2,768,256]{2,1,0:T(8,128)(2,1)S(1)}, u32[]{:S(2)}, u32[]{:S(2)}) collective-permute-start(bf16[2,768,256]{2,1,0:T(8,128)(2,1)} %get-tuple-element.284), channel_id=1, source_target_pairs={{0,4},{4,0},{8,12},{12,8},{16,20},{20,16},{24,28},{28,24},{1,5},{5... | collective-permute-start | bytes 2359304 | tf_op jit(solution)/shard_map/ppermute | solution.py:333
  12.4 2.3 %shard_map.122 = (s32[128]{0:T(128)S(1)}, s32[8,128]{1,0:T(8,128)S(1)}, s32[1]{0:T(128)}) custom-call(s32[128]{0:T(128)} %get-tuple-element.269.log_ref, s32[8,128]{1,0:T(8,128)} %get-tuple-element.270.state_ref), custom_call_target="tpu_custom_call" | custom-call | flops 1000 | bytes 1000 | tf_op jit(solution)/shard_map/pallas_call | solution.py:217
  14.8 17.7 %shard_map.123 = (f32[2,256,1024]{2,1,0:T(8,128)}, f32[2,256,1024]{2,1,0:T(8,128)}) custom-call(s32[8]{0:T(128)} %length_ref, bf16[8,32,2048]{2,1,0:T(8,128)(2,1)} %query_ref, bf16[8,2,32,256]{3,2,1,0:T(8,128)(2,1)} %new_ref, bf16[8,2,768,256]{3,2,1,0:T(8,128)(2,1)} %cache_ref.10, bf16[2048,4096]{1,0:T(8,128)(2,1)} %weight_ref), custom_call_target="tpu_custom_call" | custom-call | flops 1000 | bytes 1000 | tf_op jit(solution)/shard_map/pallas_call | solution.py:585
  32.6 2.2 %shard_map.124 = (bf16[1,768,256]{2,1,0:T(8,128)(2,1)}, bf16[1,768,256]{2,1,0:T(8,128)(2,1)}, bf16[1,768,256]{2,1,0:T(8,128)(2,1)}) custom-call(s32[32]{0:T(128)S(1)} %copy-done.1, s32[128]{0:T(128)S(1)} %get-tuple-element.463.log_ref, bf16[8,2,768,256]{3,2,1,0:T(8,128)(2,1)} %refs_5_.1, bf16[2,768,256]{2,1,0:T(8,128)(2,1)S(1)} %collective-permute-done.3.refs_0_.refs_6_, ...), custom_call_target="tpu_custom_call" | custom-call | flops 1000 | bytes 1000 | tf_op jit(solution)/shard_map/pallas_call | solution.py:242
  34.9 5.5 %collective-permute-start.6 = (bf16[1,768,256]{2,1,0:T(8,128)(2,1)}, bf16[1,768,256]{2,1,0:T(8,128)(2,1)S(1)}, u32[]{:S(2)}, u32[]{:S(2)}) collective-permute-start(bf16[1,768,256]{2,1,0:T(8,128)(2,1)} %get-tuple-element.295), channel_id=1, source_target_pairs={{0,8},{4,12},{8,16},{12,20},{16,24},{20,28},{1,9},{5,13},{9,17},{1... | collective-permute-start | bytes 1179656 | tf_op jit(solution)/shard_map/ppermute | solution.py:331
  40.4 1.3 collective-permute-start.7
  42.2 2.8 %shard_map.125 = (bf16[1,768,256]{2,1,0:T(8,128)(2,1)}, bf16[1,768,256]{2,1,0:T(8,128)(2,1)}, bf16[1,768,256]{2,1,0:T(8,128)(2,1)}) custom-call(s32[32]{0:T(128)S(1)} %copy-done.1, s32[128]{0:T(128)S(1)} %get-tuple-element.463.log_ref, bf16[8,2,768,256]{3,2,1,0:T(8,128)(2,1)} %refs_5_.1, bf16[2,768,256]{2,1,0:T(8,128)(2,1)S(1)} %collective-permute-done.3.refs_0_.refs_6_, ...), custom_call_target="tpu_custom_call" | custom-call | flops 1000 | bytes 1000 | tf_op jit(solution)/shard_map/pallas_call | solution.py:242
  45.0 4.6 %collective-permute-start.11 = (bf16[1,768,256]{2,1,0:T(8,128)(2,1)}, bf16[1,768,256]{2,1,0:T(8,128)(2,1)S(1)}, u32[]{:S(2)}, u32[]{:S(2)}) collective-permute-start(bf16[1,768,256]{2,1,0:T(8,128)(2,1)} %get-tuple-element.314), channel_id=1, source_target_pairs={{0,8},{4,12},{8,16},{12,20},{16,24},{20,28},{1,9},{5,13},{9,17},{1... | collective-permute-start | bytes 1179656 | tf_op jit(solution)/shard_map/ppermute | solution.py:331
  49.7 1.3 collective-permute-start.12
  50.9 2.7 %collective-permute-done.7.refs_4_.refs_10_ = bf16[1,768,256]{2,1,0:T(8,128)(2,1)S(1)} collective-permute-done((bf16[1,768,256]{2,1,0:T(8,128)(2,1)}, bf16[1,768,256]{2,1,0:T(8,128)(2,1)S(1)}, u32[]{:S(2)}, u32[]{:S(2)}) %collective-permute-start.7) | collective-permute-done | bytes 393248 | tf_op jit(solution)/shard_map/ppermute | solution.py:332
  54.2 2.8 %shard_map.126 = (bf16[1,768,256]{2,1,0:T(8,128)(2,1)}, bf16[1,768,256]{2,1,0:T(8,128)(2,1)}, bf16[1,768,256]{2,1,0:T(8,128)(2,1)}) custom-call(s32[32]{0:T(128)S(1)} %copy-done.1, s32[128]{0:T(128)S(1)} %get-tuple-element.463.log_ref, bf16[8,2,768,256]{3,2,1,0:T(8,128)(2,1)} %refs_5_.1, bf16[2,768,256]{2,1,0:T(8,128)(2,1)S(1)} %collective-permute-done.3.refs_0_.refs_6_, ...), custom_call_target="tpu_custom_call" | custom-call | flops 1000 | bytes 1000 | tf_op jit(solution)/shard_map/pallas_call | solution.py:242
  57.0 4.4 %collective-permute-start.14 = (bf16[1,768,256]{2,1,0:T(8,128)(2,1)}, bf16[1,768,256]{2,1,0:T(8,128)(2,1)}, u32[]{:S(2)}, u32[]{:S(2)}) collective-permute-start(bf16[1,768,256]{2,1,0:T(8,128)(2,1)} %get-tuple-element.321), channel_id=1, source_target_pairs={{0,8},{4,12},{8,16},{12,20},{16,24},{20,28},{1,9},{5,13},{9,17},{1... | collective-permute-start | bytes 1179656 | tf_op jit(solution)/shard_map/ppermute | solution.py:331
  61.4 3.3 %shard_map.127 = (f32[256,1024]{1,0:T(8,128)}, bf16[256,1024]{1,0:T(8,128)(2,1)}) custom-call(f32[2,256,1024]{2,1,0:T(8,128)} %get-tuple-element.305.keep_ref, f32[2,256,1024]{2,1,0:T(8,128)} %collective-permute-done.9.got_ref), custom_call_target="tpu_custom_call" | custom-call | flops 1000 | bytes 1000 | tf_op jit(solution)/shard_map/pallas_call | solution.py:626
  64.7 1.3 collective-permute-start.15
  66.0 0.8 collective-permute-start.16
  66.8 2.4 %shard_map.128 = (bf16[1,768,256]{2,1,0:T(8,128)(2,1)}, bf16[1,768,256]{2,1,0:T(8,128)(2,1)}, bf16[1,768,256]{2,1,0:T(8,128)(2,1)}) custom-call(s32[32]{0:T(128)S(1)} %copy-done.1, s32[128]{0:T(128)S(1)} %get-tuple-element.463.log_ref, bf16[8,2,768,256]{3,2,1,0:T(8,128)(2,1)} %refs_5_.1, bf16[2,768,256]{2,1,0:T(8,128)(2,1)S(1)} %collective-permute-done.3.refs_0_.refs_6_, ...), custom_call_target="tpu_custom_call" | custom-call | flops 1000 | bytes 1000 | tf_op jit(solution)/shard_map/pallas_call | solution.py:242
  69.3 5.8 %collective-permute-start.17 = (bf16[1,768,256]{2,1,0:T(8,128)(2,1)}, bf16[1,768,256]{2,1,0:T(8,128)(2,1)}, u32[]{:S(2)}, u32[]{:S(2)}) collective-permute-start(bf16[1,768,256]{2,1,0:T(8,128)(2,1)} %get-tuple-element.328), channel_id=1, source_target_pairs={{0,8},{4,12},{8,16},{12,20},{16,24},{20,28},{1,9},{5,13},{9,17},{1... | collective-permute-start | bytes 1179656 | tf_op jit(solution)/shard_map/ppermute | solution.py:331
  75.1 1.3 collective-permute-start.18
  76.4 1.0 collective-permute-start.19
  77.5 2.7 %shard_map.129 = (bf16[1,768,256]{2,1,0:T(8,128)(2,1)}, bf16[1,768,256]{2,1,0:T(8,128)(2,1)}, bf16[1,768,256]{2,1,0:T(8,128)(2,1)}) custom-call(s32[32]{0:T(128)S(1)} %copy-done.1, s32[128]{0:T(128)S(1)} %get-tuple-element.463.log_ref, bf16[8,2,768,256]{3,2,1,0:T(8,128)(2,1)} %refs_5_.1, bf16[2,768,256]{2,1,0:T(8,128)(2,1)S(1)} %collective-permute-done.3.refs_0_.refs_6_, ...), custom_call_target="tpu_custom_call" | custom-call | flops 1000 | bytes 1000 | tf_op jit(solution)/shard_map/pallas_call | solution.py:242
  80.2 5.7 %collective-permute-start.20 = (bf16[1,768,256]{2,1,0:T(8,128)(2,1)}, bf16[1,768,256]{2,1,0:T(8,128)(2,1)}, u32[]{:S(2)}, u32[]{:S(2)}) collective-permute-start(bf16[1,768,256]{2,1,0:T(8,128)(2,1)} %get-tuple-element.335), channel_id=1, source_target_pairs={{0,8},{4,12},{8,16},{12,20},{16,24},{20,28},{1,9},{5,13},{9,17},{1... | collective-permute-start | bytes 1179656 | tf_op jit(solution)/shard_map/ppermute | solution.py:331
  85.9 1.3 collective-permute-start.21
  88.0 1.5 collective-permute-start.10
  89.5 2.7 %shard_map.130 = (bf16[1,768,256]{2,1,0:T(8,128)(2,1)}, bf16[1,768,256]{2,1,0:T(8,128)(2,1)}, bf16[1,768,256]{2,1,0:T(8,128)(2,1)}) custom-call(s32[32]{0:T(128)S(1)} %copy-done.1, s32[128]{0:T(128)S(1)} %get-tuple-element.463.log_ref, bf16[8,2,768,256]{3,2,1,0:T(8,128)(2,1)} %refs_5_.1, bf16[2,768,256]{2,1,0:T(8,128)(2,1)S(1)} %collective-permute-done.3.refs_0_.refs_6_, ...), custom_call_target="tpu_custom_call" | custom-call | flops 1000 | bytes 1000 | tf_op jit(solution)/shard_map/pallas_call | solution.py:242
  92.2 5.2 %collective-permute-start.23 = (bf16[1,768,256]{2,1,0:T(8,128)(2,1)}, bf16[1,768,256]{2,1,0:T(8,128)(2,1)}, u32[]{:S(2)}, u32[]{:S(2)}) collective-permute-start(bf16[1,768,256]{2,1,0:T(8,128)(2,1)} %get-tuple-element.342), channel_id=1, source_target_pairs={{0,8},{4,12},{8,16},{12,20},{16,24},{20,28},{1,9},{5,13},{9,17},{1... | collective-permute-start | bytes 1179656 | tf_op jit(solution)/shard_map/ppermute | solution.py:331
  97.4 1.3 collective-permute-start.24
  98.7 1.3 collective-permute-start.25
  100.0 0.9 shard_map.131
  101.0 6.3 %collective-permute-start.29 = (bf16[1,768,256]{2,1,0:T(8,128)(2,1)}, bf16[1,768,256]{2,1,0:T(8,128)(2,1)}, u32[]{:S(2)}, u32[]{:S(2)}) collective-permute-start(bf16[1,768,256]{2,1,0:T(8,128)(2,1)} %get-tuple-element.353), channel_id=1, source_target_pairs={{0,8},{4,12},{8,16},{12,20},{16,24},{20,28},{1,9},{5,13},{9,17},{1... | collective-permute-start | bytes 1179656 | tf_op jit(solution)/shard_map/ppermute | solution.py:331
  107.3 1.3 collective-permute-start.30
  108.6 1.6 %collective-permute-start.31 = (bf16[1,768,256]{2,1,0:T(8,128)(2,1)}, bf16[1,768,256]{2,1,0:T(8,128)(2,1)}, u32[]{:S(2)}, u32[]{:S(2)}) collective-permute-start(bf16[1,768,256]{2,1,0:T(8,128)(2,1)} %get-tuple-element.355), channel_id=1, source_target_pairs={{0,4},{4,0},{8,12},{12,8},{16,20},{20,16},{24,28},{28,24},{1,5},{5... | collective-permute-start | bytes 1179656 | tf_op jit(solution)/shard_map/ppermute | solution.py:333
  110.2 1.0 shard_map.132
  111.1 5.3 %collective-permute-start.26 = (bf16[1,768,256]{2,1,0:T(8,128)(2,1)}, bf16[1,768,256]{2,1,0:T(8,128)(2,1)}, u32[]{:S(2)}, u32[]{:S(2)}) collective-permute-start(bf16[1,768,256]{2,1,0:T(8,128)(2,1)} %get-tuple-element.350), channel_id=1, source_target_pairs={{0,8},{4,12},{8,16},{12,20},{16,24},{20,28},{1,9},{5,13},{9,17},{1... | collective-permute-start | bytes 1179656 | tf_op jit(solution)/shard_map/ppermute | solution.py:331
  116.5 1.3 collective-permute-start.27
  117.8 2.3 %collective-permute-start.28 = (bf16[1,768,256]{2,1,0:T(8,128)(2,1)}, bf16[1,768,256]{2,1,0:T(8,128)(2,1)}, u32[]{:S(2)}, u32[]{:S(2)}) collective-permute-start(bf16[1,768,256]{2,1,0:T(8,128)(2,1)} %get-tuple-element.352), channel_id=1, source_target_pairs={{0,4},{4,0},{8,12},{12,8},{16,20},{20,16},{24,28},{28,24},{1,5},{5... | collective-permute-start | bytes 1179656 | tf_op jit(solution)/shard_map/ppermute | solution.py:333
  120.1 2.3 %add_convert_fusion = bf16[256,1024]{1,0:T(8,128)(2,1)} fusion(f32[256,1024]{1,0:T(8,128)} %get-tuple-element.309, bf16[256,1024]{1,0:T(8,128)(2,1)} %collective-permute-done.10), kind=kLoop, calls=%fused_computation | loop fusion | flops 786432 | bytes 2097152 | tf_op jit(solution)/shard_map/convert_element_type | solution.py:436
  122.4 4.1 %collective-permute-done.27 = bf16[1,768,256]{2,1,0:T(8,128)(2,1)} collective-permute-done((bf16[1,768,256]{2,1,0:T(8,128)(2,1)}, bf16[1,768,256]{2,1,0:T(8,128)(2,1)}, u32[]{:S(2)}, u32[]{:S(2)}) %collective-permute-start.27) | collective-permute-done | bytes 393248 | tf_op jit(solution)/shard_map/ppermute | solution.py:332
  126.4 20.6 %while.19 = (s32[1]{0:T(128)}, s32[128]{0:T(128)S(1)}, s32[8,128]{1,0:T(8,128)S(1)}, bf16[1,768,256]{2,1,0:T(8,128)(2,1)}, bf16[1,768,256]{2,1,0:T(8,128)(2,1)},...) while((s32[1]{0:T(128)}, s32[128]{0:T(128)S(1)}, ...), condition=%region_1.0_spmd, body=%region_0.0_spmd | while | flops 1001 | bytes 4729201 | solution.py:448
  128.2 3.1 %body.1 = (s32[128]{0:T(128)S(1)}, s32[8,128]{1,0:T(8,128)S(1)}, s32[1]{0:T(128)}, bf16[1,768,256]{2,1,0:T(8,128)(2,1)}, bf16[1,768,256]{2,1,0:T(8,128)(2,1)}, /...) custom-call(s32[32]{0:T(128)S(1)} %get-tuple-element.535.source_ref, ...), custom_call_target="tpu_custom_call", output_to_operand_aliasing={{6}: (31, {})} | custom-call | flops 1000 | bytes 1000 | tf_op jit(solution)/shard_map/while/body/pallas_call | solution.py:296
  131.3 5.1 %collective-permute-start = (bf16[1,768,256]{2,1,0:T(8,128)(2,1)}, bf16[1,768,256]{2,1,0:T(8,128)(2,1)}, u32[]{:S(2)}, u32[]{:S(2)}) collective-permute-start(bf16[1,768,256]{2,1,0:T(8,128)(2,1)} %get-tuple-element.167), channel_id=1, source_target_pairs={{0,8},{4,12},{8,16},{12,20},{16,24},{20,28},{1,9},{5,13},{9,17},{1... | collective-permute-start | bytes 1179656 | tf_op jit(solution)/shard_map/while/body/ppermute | solution.py:331
  136.4 1.3 collective-permute-start.1
  137.7 2.7 %collective-permute-start.2 = (bf16[1,768,256]{2,1,0:T(8,128)(2,1)}, bf16[1,768,256]{2,1,0:T(8,128)(2,1)}, u32[]{:S(2)}, u32[]{:S(2)}) collective-permute-start(bf16[1,768,256]{2,1,0:T(8,128)(2,1)} %get-tuple-element.169), channel_id=1, source_target_pairs={{0,4},{4,0},{8,12},{12,8},{16,20},{20,16},{24,28},{28,24},{1,5},{5... | collective-permute-start | bytes 1179656 | tf_op jit(solution)/shard_map/while/body/ppermute | solution.py:333
  140.4 0.8 collective-permute-done
  141.2 5.1 %collective-permute-done.1 = bf16[1,768,256]{2,1,0:T(8,128)(2,1)} collective-permute-done((bf16[1,768,256]{2,1,0:T(8,128)(2,1)}, bf16[1,768,256]{2,1,0:T(8,128)(2,1)}, u32[]{:S(2)}, u32[]{:S(2)}) %collective-permute-start.1) | collective-permute-done | bytes 393248 | tf_op jit(solution)/shard_map/while/body/ppermute | solution.py:332
  147.0 5.9 %shard_map.134 = (bf16[4,2,768,256]{3,2,1,0:T(8,128)(2,1)}, bf16[4,2048]{1,0:T(4,128)(2,1)}) custom-call(s32[32]{0:T(128)S(1)} %get-tuple-element.576, s32[64]{0:T(128)} %refs_1_.1, s32[128]{0:T(128)S(1)} %get-tuple-element.356.refs_2_, bf16[4,2048]{1,0:T(4,128)(2,1)} %refs_3_.1, bf16[4,2,256]{2,1,0:T(2,128)(2,1)} %refs_4_.1, ...), custom_call_target="tpu_custom_call" | custom-call | flops 1000 | bytes 1000 | tf_op jit(solution)/shard_map/pallas_call | solution.py:396
  (39 shorter events, 3.4 us)
Async XLA Ops:
  0.6 31.9 %copy-start.1 = (s32[32]{0:T(128)S(1)}, s32[32]{0:T(128)}, u32[]{:S(2)}) copy-start(s32[32]{0:T(128)} %refs_0_.1) | copy-start | bytes 388
  4.6 28.0 %collective-permute-start.3 = (bf16[2,768,256]{2,1,0:T(8,128)(2,1)}, bf16[2,768,256]{2,1,0:T(8,128)(2,1)S(1)}, u32[]{:S(2)}, u32[]{:S(2)}) collective-permute-start(bf16[2,768,256]{2,1,0:T(8,128)(2,1)} %get-tuple-element.282), channel_id=1, source_target_pairs={{0,8},{4,12},{8,16},{12,20},{16,24},{20,28},{1,9},{5,13},{9,17},{1... | collective-permute-start | bytes 2359304 | tf_op jit(solution)/shard_map/ppermute | solution.py:331
  9.5 23.0 %collective-permute-start.4 = (bf16[2,768,256]{2,1,0:T(8,128)(2,1)}, bf16[2,768,256]{2,1,0:T(8,128)(2,1)S(1)}, u32[]{:S(2)}, u32[]{:S(2)}) collective-permute-start(bf16[2,768,256]{2,1,0:T(8,128)(2,1)} %get-tuple-element.283), channel_id=1, source_target_pairs={{8,0},{12,4},{16,8},{20,12},{24,16},{28,20},{9,1},{13,5},{17,9},{2... | collective-permute-start | bytes 2359304 | tf_op jit(solution)/shard_map/ppermute | solution.py:332
  10.8 21.7 %collective-permute-start.5 = (bf16[2,768,256]{2,1,0:T(8,128)(2,1)}, bf16[2,768,256]{2,1,0:T(8,128)(2,1)S(1)}, u32[]{:S(2)}, u32[]{:S(2)}) collective-permute-start(bf16[2,768,256]{2,1,0:T(8,128)(2,1)} %get-tuple-element.284), channel_id=1, source_target_pairs={{0,4},{4,0},{8,12},{12,8},{16,20},{20,16},{24,28},{28,24},{1,5},{5... | collective-permute-start | bytes 2359304 | tf_op jit(solution)/shard_map/ppermute | solution.py:333
  34.8 26.6 %collective-permute-start.9 = (f32[2,256,1024]{2,1,0:T(8,128)}, f32[2,256,1024]{2,1,0:T(8,128)}, u32[]{:S(2)}, u32[]{:S(2)}) collective-permute-start(f32[2,256,1024]{2,1,0:T(8,128)} %get-tuple-element.303), channel_id=1, source_target_pairs={{0,1},{1,0},{2,3},{3,2},{4,5},{5,4},{6,7},{7,6},{8,9},{9,8},{10,11... | collective-permute-start | bytes 6291464 | tf_op jit(solution)/shard_map/ppermute | solution.py:429
  34.9 14.8 %collective-permute-start.6 = (bf16[1,768,256]{2,1,0:T(8,128)(2,1)}, bf16[1,768,256]{2,1,0:T(8,128)(2,1)S(1)}, u32[]{:S(2)}, u32[]{:S(2)}) collective-permute-start(bf16[1,768,256]{2,1,0:T(8,128)(2,1)} %get-tuple-element.295), channel_id=1, source_target_pairs={{0,8},{4,12},{8,16},{12,20},{16,24},{20,28},{1,9},{5,13},{9,17},{1... | collective-permute-start | bytes 1179656 | tf_op jit(solution)/shard_map/ppermute | solution.py:331
  40.4 13.3 %collective-permute-start.7 = (bf16[1,768,256]{2,1,0:T(8,128)(2,1)}, bf16[1,768,256]{2,1,0:T(8,128)(2,1)S(1)}, u32[]{:S(2)}, u32[]{:S(2)}) collective-permute-start(bf16[1,768,256]{2,1,0:T(8,128)(2,1)} %get-tuple-element.296), channel_id=1, source_target_pairs={{8,0},{12,4},{16,8},{20,12},{24,16},{28,20},{9,1},{13,5},{17,9},{2... | collective-permute-start | bytes 1179656 | tf_op jit(solution)/shard_map/ppermute | solution.py:332
  41.7 12.5 %collective-permute-start.8 = (bf16[1,768,256]{2,1,0:T(8,128)(2,1)}, bf16[1,768,256]{2,1,0:T(8,128)(2,1)S(1)}, u32[]{:S(2)}, u32[]{:S(2)}) collective-permute-start(bf16[1,768,256]{2,1,0:T(8,128)(2,1)} %get-tuple-element.297), channel_id=1, source_target_pairs={{0,4},{4,0},{8,12},{12,8},{16,20},{20,16},{24,28},{28,24},{1,5},{5... | collective-permute-start | bytes 1179656 | tf_op jit(solution)/shard_map/ppermute | solution.py:333
  45.0 21.0 %collective-permute-start.11 = (bf16[1,768,256]{2,1,0:T(8,128)(2,1)}, bf16[1,768,256]{2,1,0:T(8,128)(2,1)S(1)}, u32[]{:S(2)}, u32[]{:S(2)}) collective-permute-start(bf16[1,768,256]{2,1,0:T(8,128)(2,1)} %get-tuple-element.314), channel_id=1, source_target_pairs={{0,8},{4,12},{8,16},{12,20},{16,24},{20,28},{1,9},{5,13},{9,17},{1... | collective-permute-start | bytes 1179656 | tf_op jit(solution)/shard_map/ppermute | solution.py:331
  49.7 17.2 %collective-permute-start.12 = (bf16[1,768,256]{2,1,0:T(8,128)(2,1)}, bf16[1,768,256]{2,1,0:T(8,128)(2,1)}, u32[]{:S(2)}, u32[]{:S(2)}) collective-permute-start(bf16[1,768,256]{2,1,0:T(8,128)(2,1)} %get-tuple-element.315), channel_id=1, source_target_pairs={{8,0},{12,4},{16,8},{20,12},{24,16},{28,20},{9,1},{13,5},{17,9},{2... | collective-permute-start | bytes 1179656 | tf_op jit(solution)/shard_map/ppermute | solution.py:332
  53.7 13.2 %collective-permute-start.13 = (bf16[1,768,256]{2,1,0:T(8,128)(2,1)}, bf16[1,768,256]{2,1,0:T(8,128)(2,1)}, u32[]{:S(2)}, u32[]{:S(2)}) collective-permute-start(bf16[1,768,256]{2,1,0:T(8,128)(2,1)} %get-tuple-element.316), channel_id=1, source_target_pairs={{0,4},{4,0},{8,12},{12,8},{16,20},{20,16},{24,28},{28,24},{1,5},{5... | collective-permute-start | bytes 1179656 | tf_op jit(solution)/shard_map/ppermute | solution.py:333
  57.0 19.5 %collective-permute-start.14 = (bf16[1,768,256]{2,1,0:T(8,128)(2,1)}, bf16[1,768,256]{2,1,0:T(8,128)(2,1)}, u32[]{:S(2)}, u32[]{:S(2)}) collective-permute-start(bf16[1,768,256]{2,1,0:T(8,128)(2,1)} %get-tuple-element.321), channel_id=1, source_target_pairs={{0,8},{4,12},{8,16},{12,20},{16,24},{20,28},{1,9},{5,13},{9,17},{1... | collective-permute-start | bytes 1179656 | tf_op jit(solution)/shard_map/ppermute | solution.py:331
  64.7 12.8 %collective-permute-start.15 = (bf16[1,768,256]{2,1,0:T(8,128)(2,1)}, bf16[1,768,256]{2,1,0:T(8,128)(2,1)}, u32[]{:S(2)}, u32[]{:S(2)}) collective-permute-start(bf16[1,768,256]{2,1,0:T(8,128)(2,1)} %get-tuple-element.322), channel_id=1, source_target_pairs={{8,0},{12,4},{16,8},{20,12},{24,16},{28,20},{9,1},{13,5},{17,9},{2... | collective-permute-start | bytes 1179656 | tf_op jit(solution)/shard_map/ppermute | solution.py:332
  66.0 44.2 %copy-start = (bf16[1,768,256]{2,1,0:T(8,128)(2,1)}, bf16[1,768,256]{2,1,0:T(8,128)(2,1)S(1)}, u32[]{:S(2)}) copy-start(bf16[1,768,256]{2,1,0:T(8,128)(2,1)S(1)} %collective-permute-done.11.refs_6_.refs_12_) | copy-start | bytes 1179652
  66.0 11.5 %collective-permute-start.16 = (bf16[1,768,256]{2,1,0:T(8,128)(2,1)}, bf16[1,768,256]{2,1,0:T(8,128)(2,1)}, u32[]{:S(2)}, u32[]{:S(2)}) collective-permute-start(bf16[1,768,256]{2,1,0:T(8,128)(2,1)} %get-tuple-element.323), channel_id=1, source_target_pairs={{0,4},{4,0},{8,12},{12,8},{16,20},{20,16},{24,28},{28,24},{1,5},{5... | collective-permute-start | bytes 1179656 | tf_op jit(solution)/shard_map/ppermute | solution.py:333
  69.3 17.8 %collective-permute-start.17 = (bf16[1,768,256]{2,1,0:T(8,128)(2,1)}, bf16[1,768,256]{2,1,0:T(8,128)(2,1)}, u32[]{:S(2)}, u32[]{:S(2)}) collective-permute-start(bf16[1,768,256]{2,1,0:T(8,128)(2,1)} %get-tuple-element.328), channel_id=1, source_target_pairs={{0,8},{4,12},{8,16},{12,20},{16,24},{20,28},{1,9},{5,13},{9,17},{1... | collective-permute-start | bytes 1179656 | tf_op jit(solution)/shard_map/ppermute | solution.py:331
  75.1 12.9 %collective-permute-start.18 = (bf16[1,768,256]{2,1,0:T(8,128)(2,1)}, bf16[1,768,256]{2,1,0:T(8,128)(2,1)}, u32[]{:S(2)}, u32[]{:S(2)}) collective-permute-start(bf16[1,768,256]{2,1,0:T(8,128)(2,1)} %get-tuple-element.329), channel_id=1, source_target_pairs={{8,0},{12,4},{16,8},{20,12},{24,16},{28,20},{9,1},{13,5},{17,9},{2... | collective-permute-start | bytes 1179656 | tf_op jit(solution)/shard_map/ppermute | solution.py:332
  76.4 13.1 %collective-permute-start.19 = (bf16[1,768,256]{2,1,0:T(8,128)(2,1)}, bf16[1,768,256]{2,1,0:T(8,128)(2,1)}, u32[]{:S(2)}, u32[]{:S(2)}) collective-permute-start(bf16[1,768,256]{2,1,0:T(8,128)(2,1)} %get-tuple-element.330), channel_id=1, source_target_pairs={{0,4},{4,0},{8,12},{12,8},{16,20},{20,16},{24,28},{28,24},{1,5},{5... | collective-permute-start | bytes 1179656 | tf_op jit(solution)/shard_map/ppermute | solution.py:333
  80.2 17.2 %collective-permute-start.20 = (bf16[1,768,256]{2,1,0:T(8,128)(2,1)}, bf16[1,768,256]{2,1,0:T(8,128)(2,1)}, u32[]{:S(2)}, u32[]{:S(2)}) collective-permute-start(bf16[1,768,256]{2,1,0:T(8,128)(2,1)} %get-tuple-element.335), channel_id=1, source_target_pairs={{0,8},{4,12},{8,16},{12,20},{16,24},{20,28},{1,9},{5,13},{9,17},{1... | collective-permute-start | bytes 1179656 | tf_op jit(solution)/shard_map/ppermute | solution.py:331
  85.9 12.8 %collective-permute-start.21 = (bf16[1,768,256]{2,1,0:T(8,128)(2,1)}, bf16[1,768,256]{2,1,0:T(8,128)(2,1)}, u32[]{:S(2)}, u32[]{:S(2)}) collective-permute-start(bf16[1,768,256]{2,1,0:T(8,128)(2,1)} %get-tuple-element.336), channel_id=1, source_target_pairs={{8,0},{12,4},{16,8},{20,12},{24,16},{28,20},{9,1},{13,5},{17,9},{2... | collective-permute-start | bytes 1179656 | tf_op jit(solution)/shard_map/ppermute | solution.py:332
  87.1 12.9 %collective-permute-start.22 = (bf16[1,768,256]{2,1,0:T(8,128)(2,1)}, bf16[1,768,256]{2,1,0:T(8,128)(2,1)}, u32[]{:S(2)}, u32[]{:S(2)}) collective-permute-start(bf16[1,768,256]{2,1,0:T(8,128)(2,1)} %get-tuple-element.337), channel_id=1, source_target_pairs={{0,4},{4,0},{8,12},{12,8},{16,20},{20,16},{24,28},{28,24},{1,5},{5... | collective-permute-start | bytes 1179656 | tf_op jit(solution)/shard_map/ppermute | solution.py:333
  88.0 28.5 %collective-permute-start.10 = (bf16[256,1024]{1,0:T(8,128)(2,1)}, bf16[256,1024]{1,0:T(8,128)(2,1)}, u32[]{:S(2)}, u32[]{:S(2)}) collective-permute-start(bf16[256,1024]{1,0:T(8,128)(2,1)} %get-tuple-element.310), channel_id=1, source_target_pairs={{0,2},{2,0},{1,3},{3,1},{4,6},{6,4},{5,7},{7,5},{8,10},{10,8},{9,1... | collective-permute-start | bytes 1572872 | tf_op jit(solution)/shard_map/ppermute | solution.py:434
  92.2 15.1 %collective-permute-start.23 = (bf16[1,768,256]{2,1,0:T(8,128)(2,1)}, bf16[1,768,256]{2,1,0:T(8,128)(2,1)}, u32[]{:S(2)}, u32[]{:S(2)}) collective-permute-start(bf16[1,768,256]{2,1,0:T(8,128)(2,1)} %get-tuple-element.342), channel_id=1, source_target_pairs={{0,8},{4,12},{8,16},{12,20},{16,24},{20,28},{1,9},{5,13},{9,17},{1... | collective-permute-start | bytes 1179656 | tf_op jit(solution)/shard_map/ppermute | solution.py:331
  97.4 11.2 %collective-permute-start.24 = (bf16[1,768,256]{2,1,0:T(8,128)(2,1)}, bf16[1,768,256]{2,1,0:T(8,128)(2,1)}, u32[]{:S(2)}, u32[]{:S(2)}) collective-permute-start(bf16[1,768,256]{2,1,0:T(8,128)(2,1)} %get-tuple-element.343), channel_id=1, source_target_pairs={{8,0},{12,4},{16,8},{20,12},{24,16},{28,20},{9,1},{13,5},{17,9},{2... | collective-permute-start | bytes 1179656 | tf_op jit(solution)/shard_map/ppermute | solution.py:332
  98.7 11.5 %collective-permute-start.25 = (bf16[1,768,256]{2,1,0:T(8,128)(2,1)}, bf16[1,768,256]{2,1,0:T(8,128)(2,1)}, u32[]{:S(2)}, u32[]{:S(2)}) collective-permute-start(bf16[1,768,256]{2,1,0:T(8,128)(2,1)} %get-tuple-element.344), channel_id=1, source_target_pairs={{0,4},{4,0},{8,12},{12,8},{16,20},{20,16},{24,28},{28,24},{1,5},{5... | collective-permute-start | bytes 1179656 | tf_op jit(solution)/shard_map/ppermute | solution.py:333
  101.0 16.8 %collective-permute-start.29 = (bf16[1,768,256]{2,1,0:T(8,128)(2,1)}, bf16[1,768,256]{2,1,0:T(8,128)(2,1)}, u32[]{:S(2)}, u32[]{:S(2)}) collective-permute-start(bf16[1,768,256]{2,1,0:T(8,128)(2,1)} %get-tuple-element.353), channel_id=1, source_target_pairs={{0,8},{4,12},{8,16},{12,20},{16,24},{20,28},{1,9},{5,13},{9,17},{1... | collective-permute-start | bytes 1179656 | tf_op jit(solution)/shard_map/ppermute | solution.py:331
  107.3 15.1 %collective-permute-start.30 = (bf16[1,768,256]{2,1,0:T(8,128)(2,1)}, bf16[1,768,256]{2,1,0:T(8,128)(2,1)}, u32[]{:S(2)}, u32[]{:S(2)}) collective-permute-start(bf16[1,768,256]{2,1,0:T(8,128)(2,1)} %get-tuple-element.354), channel_id=1, source_target_pairs={{8,0},{12,4},{16,8},{20,12},{24,16},{28,20},{9,1},{13,5},{17,9},{2... | collective-permute-start | bytes 1179656 | tf_op jit(solution)/shard_map/ppermute | solution.py:332
  108.6 13.8 %collective-permute-start.31 = (bf16[1,768,256]{2,1,0:T(8,128)(2,1)}, bf16[1,768,256]{2,1,0:T(8,128)(2,1)}, u32[]{:S(2)}, u32[]{:S(2)}) collective-permute-start(bf16[1,768,256]{2,1,0:T(8,128)(2,1)} %get-tuple-element.355), channel_id=1, source_target_pairs={{0,4},{4,0},{8,12},{12,8},{16,20},{20,16},{24,28},{28,24},{1,5},{5... | collective-permute-start | bytes 1179656 | tf_op jit(solution)/shard_map/ppermute | solution.py:333
  111.1 11.2 %collective-permute-start.26 = (bf16[1,768,256]{2,1,0:T(8,128)(2,1)}, bf16[1,768,256]{2,1,0:T(8,128)(2,1)}, u32[]{:S(2)}, u32[]{:S(2)}) collective-permute-start(bf16[1,768,256]{2,1,0:T(8,128)(2,1)} %get-tuple-element.350), channel_id=1, source_target_pairs={{0,8},{4,12},{8,16},{12,20},{16,24},{20,28},{1,9},{5,13},{9,17},{1... | collective-permute-start | bytes 1179656 | tf_op jit(solution)/shard_map/ppermute | solution.py:331
  116.5 10.0 %collective-permute-start.27 = (bf16[1,768,256]{2,1,0:T(8,128)(2,1)}, bf16[1,768,256]{2,1,0:T(8,128)(2,1)}, u32[]{:S(2)}, u32[]{:S(2)}) collective-permute-start(bf16[1,768,256]{2,1,0:T(8,128)(2,1)} %get-tuple-element.351), channel_id=1, source_target_pairs={{8,0},{12,4},{16,8},{20,12},{24,16},{28,20},{9,1},{13,5},{17,9},{2... | collective-permute-start | bytes 1179656 | tf_op jit(solution)/shard_map/ppermute | solution.py:332
  117.8 8.7 %collective-permute-start.28 = (bf16[1,768,256]{2,1,0:T(8,128)(2,1)}, bf16[1,768,256]{2,1,0:T(8,128)(2,1)}, u32[]{:S(2)}, u32[]{:S(2)}) collective-permute-start(bf16[1,768,256]{2,1,0:T(8,128)(2,1)} %get-tuple-element.352), channel_id=1, source_target_pairs={{0,4},{4,0},{8,12},{12,8},{16,20},{20,16},{24,28},{28,24},{1,5},{5... | collective-permute-start | bytes 1179656 | tf_op jit(solution)/shard_map/ppermute | solution.py:333
  131.3 9.9 %collective-permute-start = (bf16[1,768,256]{2,1,0:T(8,128)(2,1)}, bf16[1,768,256]{2,1,0:T(8,128)(2,1)}, u32[]{:S(2)}, u32[]{:S(2)}) collective-permute-start(bf16[1,768,256]{2,1,0:T(8,128)(2,1)} %get-tuple-element.167), channel_id=1, source_target_pairs={{0,8},{4,12},{8,16},{12,20},{16,24},{20,28},{1,9},{5,13},{9,17},{1... | collective-permute-start | bytes 1179656 | tf_op jit(solution)/shard_map/while/body/ppermute | solution.py:331
  136.4 10.0 %collective-permute-start.1 = (bf16[1,768,256]{2,1,0:T(8,128)(2,1)}, bf16[1,768,256]{2,1,0:T(8,128)(2,1)}, u32[]{:S(2)}, u32[]{:S(2)}) collective-permute-start(bf16[1,768,256]{2,1,0:T(8,128)(2,1)} %get-tuple-element.168), channel_id=1, source_target_pairs={{8,0},{12,4},{16,8},{20,12},{24,16},{28,20},{9,1},{13,5},{17,9},{2... | collective-permute-start | bytes 1179656 | tf_op jit(solution)/shard_map/while/body/ppermute | solution.py:332
  137.7 8.8 %collective-permute-start.2 = (bf16[1,768,256]{2,1,0:T(8,128)(2,1)}, bf16[1,768,256]{2,1,0:T(8,128)(2,1)}, u32[]{:S(2)}, u32[]{:S(2)}) collective-permute-start(bf16[1,768,256]{2,1,0:T(8,128)(2,1)} %get-tuple-element.169), channel_id=1, source_target_pairs={{0,4},{4,0},{8,12},{12,8},{16,20},{20,16},{24,28},{28,24},{1,5},{5... | collective-permute-start | bytes 1179656 | tf_op jit(solution)/shard_map/while/body/ppermute | solution.py:333
where the time goes:
time: 155 us; the launch traced here: 153 us
  starting transfers between devices  80.6 us (52%)
  Pallas kernels  53.7 us (35%)
  waiting for transfers between devices  13 us (8%)
  other arithmetic  2.3 us (1%)
    ppermute x10, starting transfers between devices, exchange(): lax.ppermute(up, 'cand', UP)  52.9 us
    pallas_call x1, Pallas kernels, reward_share(): pl.pallas_call(reward_kernel, out_shape=[jax.ShapeDtypeStruct(shape, jnp....  17.7 us
    pallas_call x8, Pallas kernels, stage(): pl.pallas_call(functools.partial(stage_kernel, turn, len(arrivals)), out_...  17.4 us
    ppermute x10, starting transfers between devices, exchange(): lax.ppermute(across, 'cand', ACROSS)  13.3 us
    ppermute x10, starting transfers between devices, exchange(): lax.ppermute(down, 'cand', DOWN)  12.8 us
    ppermute x10, waiting for transfers between devices, exchange(): lax.ppermute(down, 'cand', DOWN)  12 us
    pallas_call x1, Pallas kernels, finish(): pl.pallas_call(functools.partial(finish_kernel, len(arrivals)), out_shape...  5.85 us
    pallas_call x1, Pallas kernels, first_stage(): pl.pallas_call(first_kernel, out_shape=[jax.ShapeDtypeStruct((LOG,), jnp....  3.92 us
  transfers between devices with their start and end apart: 32, of which 6 were waited for; matrix products, arithmetic and copies ran while one was open for 1% of the time, Pallas kernels for 25%

commit v1 on v0

--- a/solution.py
+++ b/solution.py
@@ -16,9 +16,9 @@
 GRID_Z = 4
 GRID_Y = 2
 GRID = GRID_Z * GRID_Y
-ROUNDS = [(2, 1)] + [(1, 2)] * 8
+ROUNDS = [(2, 1, True)] + [(1, 2, turn not in (3, 4)) for turn in range(1, 9)]
 LAST = len(ROUNDS) - 1
-PLACE = [3 * sum(many for many, _ in ROUNDS[:turn]) for turn in range(len(ROUNDS) + 1)]
+PLACE = [3 * sum(many for many, _, _ in ROUNDS[:turn]) for turn in range(len(ROUNDS) + 1)]
 SENT = PLACE[-1]
 NEXT = 2 * SENT
 LOG = 128
@@ -37,7 +37,7 @@
 LITTLE = pl.CostEstimate(flops=1000, bytes_accessed=1000, transcendentals=0)
 
 
-def choose(state, many, lag, open_all=False):
+def choose(state, many, lag, use_across=True, open_all=False):
     z, y, wait, last_z, last_y, lane_y = state
     me = lax.axis_index("cand")
     need_z = z != last_z
@@ -50,6 +50,8 @@
     ready = move < 3
     if not open_all:
         ready = ready & (wait <= 0)
+    if not use_across:
+        ready = ready & (move != 2)
     link = jnp.where(ready, move * GRID + z * GRID_Y + y, 99)
     column = lax.broadcasted_iota(jnp.int32, (1, 128), 1)
     key = (steps * 128 + 127 - column).astype(jnp.float32)
@@ -166,7 +168,22 @@
     for i in range(SLOTS):
         owner = jnp.where((parcel >> 1) == i, source_ref[i] >> 3, owner)
     target = jnp.where(parcel < 2 * SLOTS, parcel >> 3, 0)
-    state = [owner >> 1, owner & 1, jnp.zeros_like(parcel), target >> 1, target & 1, parcel & 1]
+    aligned = []
+    crossing = {}
+    for i in range(SLOTS):
+        last_z, last_y = divmod(i // (SLOTS // GRID), GRID_Y)
+        first = source_ref[i] >> 3
+        same = (first & 1) == last_y
+        across_middle = same & (((first >> 2) == 1) != (last_z >= 2))
+        before = crossing.get((last_z >= 2, last_y), 0)
+        crossing[last_z >= 2, last_y] = before + across_middle.astype(jnp.int32)
+        aligned.append((same, across_middle, before, last_z >= 2, last_y))
+    lane = parcel & 1
+    for i, (same, across_middle, before, half, last_y) in enumerate(aligned):
+        fewer = jnp.minimum(crossing[half, 0], crossing[half, 1])
+        stays = same & jnp.logical_not(across_middle & (before >= fewer))
+        lane = jnp.where((parcel >> 1) == jnp.where(stays, i, -1), last_y, lane)
+    state = [owner >> 1, owner & 1, jnp.zeros_like(parcel), target >> 1, target & 1, lane]
     state, sent, got, _ = choose(state, *ROUNDS[0])
     begin, end = lay_out(sent, source_ref, None, cache_ref, [], (up, down, across), *scratch)
     begin()
@@ -181,7 +198,7 @@
 
 
 def first_stage(source, cache):
-    many, _ = ROUNDS[0]
+    many, _, _ = ROUNDS[0]
     log, state, *sends = pl.pallas_call(
         first_kernel,
         out_shape=[jax.ShapeDtypeStruct((LOG,), jnp.int32), jax.ShapeDtypeStruct((8, 128), jnp.int32)]
@@ -204,7 +221,7 @@
         for i in range(len(got)):
             log_out[PLACE[turn] + i] = got[i]
             log_out[SENT + PLACE[turn] + i] = sent[i]
-    state, sent, got, left = choose(state, 1, 1, True)
+    state, sent, got, left = choose(state, 1, 1, open_all=True)
     for i in range(3):
         log_out[NEXT + i] = sent[i]
         log_out[NEXT + 3 + i] = got[i]
@@ -230,7 +247,7 @@
 def stage_kernel(turn, count, source_ref, log_ref, cache_ref, *refs):
     arrivals = each_parcel(refs[:count])
     sends = refs[count : count + 3]
-    many, _ = ROUNDS[turn]
+    many, _, _ = ROUNDS[turn]
     sent = [log_ref[SENT + PLACE[turn] + i] for i in range(3 * many)]
     begin, end = lay_out(sent, source_ref, log_ref, cache_ref, arrivals, sends, *refs[count + 3 :])
     begin()
@@ -238,7 +255,7 @@
 
 
 def stage(source, log, cache, arrivals, turn):
-    many, _ = ROUNDS[turn]
+    many, _, _ = ROUNDS[turn]
     return pl.pallas_call(
         functools.partial(stage_kernel, turn, len(arrivals)),
         out_shape=sends_of(many, cache),
@@ -268,7 +285,9 @@
         parcel_from(
             sent[i], source_ref, log_ref, cache_ref, arrivals, held_in, sends[i].at[0], send_sem.at[i]
         )
-    state, next_sent, next_got, left = choose([state_ref[i : i + 1, :] for i in range(6)], 1, 1, True)
+    state, next_sent, next_got, left = choose(
+        [state_ref[i : i + 1, :] for i in range(6)], 1, 1, open_all=True
+    )
     for i in range(place):
         log_out[i] = log_ref[i]
     for i in range(3):
@@ -325,13 +344,11 @@
     )()
 
 
-def exchange(sends):
+def exchange(sends, use_across=True):
     up, down, across = sends
-    return (
-        lax.ppermute(up, "cand", UP),
-        lax.ppermute(down, "cand", DOWN),
-        lax.ppermute(across, "cand", ACROSS),
-    )
+    up = lax.ppermute(up, "cand", UP)
+    down = lax.ppermute(down, "cand", DOWN)
+    return up, down, lax.ppermute(across, "cand", ACROSS) if use_across else down
 
 
 def slot_attention(q_rows, keys, values, length, score_scale):
@@ -420,10 +437,10 @@
     give, keep = reward_share(*reward_inputs, by_core=True)
     log, give, keep = lax.optimization_barrier((log, give, keep))
     for turn in range(1, len(ROUNDS)):
-        at_hand = arrivals[: 3 * sum(sent + lag <= turn for sent, (_, lag) in enumerate(ROUNDS[:turn]))]
+        at_hand = arrivals[: 3 * sum(sent + lag <= turn for sent, (_, lag, _) in enumerate(ROUNDS[:turn]))]
         sends = stage(source, log, policy_cache, at_hand, turn)
         log, *sends = lax.optimization_barrier((log, *sends))
-        arrivals += exchange(sends)
+        arrivals += exchange(sends, ROUNDS[turn][2])
         if turn == 1:
             log, give = lax.optimization_barrier((log, give))
             give = lax.ppermute(give, "tp", [(0, 1), (1, 0), (2, 3), (3, 2)])

time: 155 us -> 131 us (0.85)
  starting transfers between devices: 80.6 us -> 69.2 us
  waiting for transfers between devices: 13 us -> 7.39 us
  Pallas kernels: 53.7 us -> 48.6 us
    ppermute x20 -> x18, starting transfers between devices: 65.7 us -> 57.5 us  [the longest x9 45.9 us: exchange(): up = lax.ppermute(up, 'cand', UP)]
    ppermute x20 -> x18, waiting for transfers between devices: 12.9 us -> 7.3 us  [the longest x9 7.28 us: exchange(): down = lax.ppermute(down, 'cand', DOWN)]
    ppermute x10 -> x7, starting transfers between devices: 13.3 us -> 10.1 us  [exchange(): lax.ppermute(across, 'cand', ACROSS)]
    pallas_call x1 -> x0, Pallas kernels: 3.07 us -> none  [late_stage(): pl.pallas_call(functools.partial(late_kernel, count), out_shape=[jax.Shap...]
    pallas_call x8, Pallas kernels: 17.4 us -> 15 us  [stage(): pl.pallas_call(functools.partial(stage_kernel, turn, len(arrivals)), out_...]
  transfers between devices with their start and end apart: 32 -> 27, of which waited for: 6 -> 3; matrix products, arithmetic and copies ran while one was open for 1% -> 2% of each run, Pallas kernels for 25% -> 27%
where the time goes in v1:
time: 131 us; the launch traced here: 129 us
  starting transfers between devices  69.2 us (53%)
  Pallas kernels  48.6 us (37%)
  waiting for transfers between devices  7.39 us (6%)
  other arithmetic  2.3 us (2%)
    ppermute x9, starting transfers between devices, exchange(): up = lax.ppermute(up, 'cand', UP)  45.9 us
    pallas_call x1, Pallas kernels, reward_share(): pl.pallas_call(reward_kernel, out_shape=[jax.ShapeDtypeStruct(shape, jnp....  17.7 us
    pallas_call x8, Pallas kernels, stage(): pl.pallas_call(functools.partial(stage_kernel, turn, len(arrivals)), out_...  15 us
    ppermute x9, starting transfers between devices, exchange(): down = lax.ppermute(down, 'cand', DOWN)  11.5 us
    ppermute x7, starting transfers between devices, exchange(): lax.ppermute(across, 'cand', ACROSS)  10.1 us
    ppermute x9, waiting for transfers between devices, exchange(): down = lax.ppermute(down, 'cand', DOWN)  7.28 us
    pallas_call x1, Pallas kernels, finish(): pl.pallas_call(functools.partial(finish_kernel, len(arrivals)), out_shape...  6.19 us
    pallas_call x1, Pallas kernels, first_stage(): pl.pallas_call(first_kernel, out_shape=[jax.ShapeDtypeStruct((LOG,), jnp....  4.07 us
  transfers between devices with their start and end apart: 27, of which 3 were waited for; matrix products, arithmetic and copies ran while one was open for 2% of the time, Pallas kernels for 27%

profile of v1, /device:TPU:0, one launch (start us, length us, event | category | flops | bytes accessed | tf_op | source)
XLA Modules:
  0.0 129.3 jit_solution(6130993795378146605)
XLA Ops:
  0.6 4.1 %shard_map.121 = (s32[128]{0:T(128)}, s32[8,128]{1,0:T(8,128)}, bf16[2,768,256]{2,1,0:T(8,128)(2,1)}, bf16[2,768,256]{2,1,0:T(8,128)(2,1)}, bf16[2,768,256]{2,1,0:T(8,128)(2,1)}) custom-call(s32[32]{0:T(128)} %refs_0_.1, bf16[8,2,768,256]{3,2,1,0:T(8,128)(2,1)} %refs_5_.1), custom_call_target="tpu_custom_call" | custom-call | flops 1000 | bytes 1000 | tf_op jit(solution)/shard_map/pallas_call | solution.py:202
  4.7 5.1 %collective-permute-start.3 = (bf16[2,768,256]{2,1,0:T(8,128)(2,1)}, bf16[2,768,256]{2,1,0:T(8,128)(2,1)S(1)}, u32[]{:S(2)}, u32[]{:S(2)}) collective-permute-start(bf16[2,768,256]{2,1,0:T(8,128)(2,1)} %get-tuple-element.268), channel_id=1, source_target_pairs={{0,8},{4,12},{8,16},{12,20},{16,24},{20,28},{1,9},{5,13},{9,17},{1... | collective-permute-start | bytes 2359304 | tf_op jit(solution)/shard_map/ppermute | solution.py:349
  9.8 1.3 collective-permute-start.4
  11.1 1.6 %collective-permute-start.5 = (bf16[2,768,256]{2,1,0:T(8,128)(2,1)}, bf16[2,768,256]{2,1,0:T(8,128)(2,1)S(1)}, u32[]{:S(2)}, u32[]{:S(2)}) collective-permute-start(bf16[2,768,256]{2,1,0:T(8,128)(2,1)} %get-tuple-element.270), channel_id=1, source_target_pairs={{0,4},{4,0},{8,12},{12,8},{16,20},{20,16},{24,28},{28,24},{1,5},{5... | collective-permute-start | bytes 2359304 | tf_op jit(solution)/shard_map/ppermute | solution.py:351
  12.7 2.3 %shard_map.122 = (s32[128]{0:T(128)S(1)}, s32[8,128]{1,0:T(8,128)S(1)}, s32[1]{0:T(128)}) custom-call(s32[128]{0:T(128)} %get-tuple-element.255.log_ref, s32[8,128]{1,0:T(8,128)} %get-tuple-element.256.state_ref), custom_call_target="tpu_custom_call" | custom-call | flops 1000 | bytes 1000 | tf_op jit(solution)/shard_map/pallas_call | solution.py:234
  15.1 17.7 %shard_map.123 = (f32[2,256,1024]{2,1,0:T(8,128)}, f32[2,256,1024]{2,1,0:T(8,128)}) custom-call(s32[8]{0:T(128)} %length_ref, bf16[8,32,2048]{2,1,0:T(8,128)(2,1)} %query_ref, bf16[8,2,32,256]{3,2,1,0:T(8,128)(2,1)} %new_ref, bf16[8,2,768,256]{3,2,1,0:T(8,128)(2,1)} %cache_ref.10, bf16[2048,4096]{1,0:T(8,128)(2,1)} %weight_ref), custom_call_target="tpu_custom_call" | custom-call | flops 1000 | bytes 1000 | tf_op jit(solution)/shard_map/pallas_call | solution.py:602
  32.8 0.0 collective-permute-done.3.refs_0_.refs_6_
  32.8 0.0 collective-permute-done.4.refs_1_.refs_7_
  32.8 2.8 %shard_map.124 = (bf16[1,768,256]{2,1,0:T(8,128)(2,1)}, bf16[1,768,256]{2,1,0:T(8,128)(2,1)}, bf16[1,768,256]{2,1,0:T(8,128)(2,1)}) custom-call(s32[32]{0:T(128)S(1)} %copy-done.2, s32[128]{0:T(128)S(1)} %get-tuple-element.439.log_ref, bf16[8,2,768,256]{3,2,1,0:T(8,128)(2,1)} %refs_5_.1, bf16[2,768,256]{2,1,0:T(8,128)(2,1)S(1)} %collective-permute-done.3.refs_0_.refs_6_, ...), custom_call_target="tpu_custom_call" | custom-call | flops 1000 | bytes 1000 | tf_op jit(solution)/shard_map/pallas_call | solution.py:259
  35.6 0.1 collective-permute-start.9
  35.7 4.9 %collective-permute-start.6 = (bf16[1,768,256]{2,1,0:T(8,128)(2,1)}, bf16[1,768,256]{2,1,0:T(8,128)(2,1)S(1)}, u32[]{:S(2)}, u32[]{:S(2)}) collective-permute-start(bf16[1,768,256]{2,1,0:T(8,128)(2,1)} %get-tuple-element.281), channel_id=1, source_target_pairs={{0,8},{4,12},{8,16},{12,20},{16,24},{20,28},{1,9},{5,13},{9,17},{1... | collective-permute-start | bytes 1179656 | tf_op jit(solution)/shard_map/ppermute | solution.py:349
  40.6 1.3 collective-permute-start.7
  41.9 0.5 collective-permute-start.8
  42.4 2.0 %shard_map.125 = (bf16[1,768,256]{2,1,0:T(8,128)(2,1)}, bf16[1,768,256]{2,1,0:T(8,128)(2,1)}, bf16[1,768,256]{2,1,0:T(8,128)(2,1)}) custom-call(s32[32]{0:T(128)S(1)} %copy-done.2, s32[128]{0:T(128)S(1)} %get-tuple-element.439.log_ref, bf16[8,2,768,256]{3,2,1,0:T(8,128)(2,1)} %refs_5_.1, bf16[2,768,256]{2,1,0:T(8,128)(2,1)S(1)} %collective-permute-done.3.refs_0_.refs_6_, ...), custom_call_target="tpu_custom_call" | custom-call | flops 1000 | bytes 1000 | tf_op jit(solution)/shard_map/pallas_call | solution.py:259
  44.4 5.6 %collective-permute-start.11 = (bf16[1,768,256]{2,1,0:T(8,128)(2,1)}, bf16[1,768,256]{2,1,0:T(8,128)(2,1)}, u32[]{:S(2)}, u32[]{:S(2)}) collective-permute-start(bf16[1,768,256]{2,1,0:T(8,128)(2,1)} %get-tuple-element.299), channel_id=1, source_target_pairs={{0,8},{4,12},{8,16},{12,20},{16,24},{20,28},{1,9},{5,13},{9,17},{1... | collective-permute-start | bytes 1179656 | tf_op jit(solution)/shard_map/ppermute | solution.py:349
  50.1 0.0 collective-permute-done.6.refs_3_.refs_9_
  50.1 1.3 collective-permute-start.12
  51.4 2.6 %collective-permute-done.7.refs_4_.refs_10_ = bf16[1,768,256]{2,1,0:T(8,128)(2,1)S(1)} collective-permute-done((bf16[1,768,256]{2,1,0:T(8,128)(2,1)}, bf16[1,768,256]{2,1,0:T(8,128)(2,1)S(1)}, u32[]{:S(2)}, u32[]{:S(2)}) %collective-permute-start.7) | collective-permute-done | bytes 393248 | tf_op jit(solution)/shard_map/ppermute | solution.py:350
  54.0 0.4 collective-permute-start.13
  54.4 2.4 %shard_map.126 = (bf16[1,768,256]{2,1,0:T(8,128)(2,1)}, bf16[1,768,256]{2,1,0:T(8,128)(2,1)}, bf16[1,768,256]{2,1,0:T(8,128)(2,1)}) custom-call(s32[32]{0:T(128)S(1)} %copy-done.2, s32[128]{0:T(128)S(1)} %get-tuple-element.439.log_ref, bf16[8,2,768,256]{3,2,1,0:T(8,128)(2,1)} %refs_5_.1, bf16[2,768,256]{2,1,0:T(8,128)(2,1)S(1)} %collective-permute-done.3.refs_0_.refs_6_, ...), custom_call_target="tpu_custom_call" | custom-call | flops 1000 | bytes 1000 | tf_op jit(solution)/shard_map/pallas_call | solution.py:259
  56.7 4.4 %collective-permute-start.14 = (bf16[1,768,256]{2,1,0:T(8,128)(2,1)}, bf16[1,768,256]{2,1,0:T(8,128)(2,1)}, u32[]{:S(2)}, u32[]{:S(2)}) collective-permute-start(bf16[1,768,256]{2,1,0:T(8,128)(2,1)} %get-tuple-element.305), channel_id=1, source_target_pairs={{0,8},{4,12},{8,16},{12,20},{16,24},{20,28},{1,9},{5,13},{9,17},{1... | collective-permute-start | bytes 1179656 | tf_op jit(solution)/shard_map/ppermute | solution.py:349
  61.1 1.3 collective-permute-start.15
  62.4 3.3 %shard_map.127 = (f32[256,1024]{1,0:T(8,128)}, bf16[256,1024]{1,0:T(8,128)(2,1)}) custom-call(f32[2,256,1024]{2,1,0:T(8,128)} %get-tuple-element.290.keep_ref, f32[2,256,1024]{2,1,0:T(8,128)} %collective-permute-done.9.got_ref), custom_call_target="tpu_custom_call" | custom-call | flops 1000 | bytes 1000 | tf_op jit(solution)/shard_map/pallas_call | solution.py:643
  65.7 2.4 %shard_map.128 = (bf16[1,768,256]{2,1,0:T(8,128)(2,1)}, bf16[1,768,256]{2,1,0:T(8,128)(2,1)}, bf16[1,768,256]{2,1,0:T(8,128)(2,1)}) custom-call(s32[32]{0:T(128)S(1)} %copy-done.2, s32[128]{0:T(128)S(1)} %get-tuple-element.439.log_ref, bf16[8,2,768,256]{3,2,1,0:T(8,128)(2,1)} %refs_5_.1, bf16[2,768,256]{2,1,0:T(8,128)(2,1)S(1)} %collective-permute-done.3.refs_0_.refs_6_, ...), custom_call_target="tpu_custom_call" | custom-call | flops 1000 | bytes 1000 | tf_op jit(solution)/shard_map/pallas_call | solution.py:259
  68.1 5.5 %collective-permute-start.16 = (bf16[1,768,256]{2,1,0:T(8,128)(2,1)}, bf16[1,768,256]{2,1,0:T(8,128)(2,1)}, u32[]{:S(2)}, u32[]{:S(2)}) collective-permute-start(bf16[1,768,256]{2,1,0:T(8,128)(2,1)} %get-tuple-element.311), channel_id=1, source_target_pairs={{0,8},{4,12},{8,16},{12,20},{16,24},{20,28},{1,9},{5,13},{9,17},{1... | collective-permute-start | bytes 1179656 | tf_op jit(solution)/shard_map/ppermute | solution.py:349
  73.7 1.3 collective-permute-start.17
  75.0 2.5 %shard_map.129 = (bf16[1,768,256]{2,1,0:T(8,128)(2,1)}, bf16[1,768,256]{2,1,0:T(8,128)(2,1)}, bf16[1,768,256]{2,1,0:T(8,128)(2,1)}) custom-call(s32[32]{0:T(128)S(1)} %copy-done.2, s32[128]{0:T(128)S(1)} %get-tuple-element.439.log_ref, bf16[8,2,768,256]{3,2,1,0:T(8,128)(2,1)} %refs_5_.1, bf16[2,768,256]{2,1,0:T(8,128)(2,1)S(1)} %collective-permute-done.3.refs_0_.refs_6_, ...), custom_call_target="tpu_custom_call" | custom-call | flops 1000 | bytes 1000 | tf_op jit(solution)/shard_map/pallas_call | solution.py:259
  77.5 6.1 %collective-permute-start.18 = (bf16[1,768,256]{2,1,0:T(8,128)(2,1)}, bf16[1,768,256]{2,1,0:T(8,128)(2,1)}, u32[]{:S(2)}, u32[]{:S(2)}) collective-permute-start(bf16[1,768,256]{2,1,0:T(8,128)(2,1)} %get-tuple-element.317), channel_id=1, source_target_pairs={{0,8},{4,12},{8,16},{12,20},{16,24},{20,28},{1,9},{5,13},{9,17},{1... | collective-permute-start | bytes 1179656 | tf_op jit(solution)/shard_map/ppermute | solution.py:349
  83.5 1.3 collective-permute-start.19
  84.8 0.1 collective-permute-start.20
  84.9 1.6 %collective-permute-start.10 = (bf16[256,1024]{1,0:T(8,128)(2,1)}, bf16[256,1024]{1,0:T(8,128)(2,1)}, u32[]{:S(2)}, u32[]{:S(2)}) collective-permute-start(bf16[256,1024]{1,0:T(8,128)(2,1)} %get-tuple-element.295), channel_id=1, source_target_pairs={{0,2},{2,0},{1,3},{3,1},{4,6},{6,4},{5,7},{7,5},{8,10},{10,8},{9,1... | collective-permute-start | bytes 1572872 | tf_op jit(solution)/shard_map/ppermute | solution.py:451
  86.5 1.0 shard_map.130
  87.4 6.2 %collective-permute-start.21 = (bf16[1,768,256]{2,1,0:T(8,128)(2,1)}, bf16[1,768,256]{2,1,0:T(8,128)(2,1)}, u32[]{:S(2)}, u32[]{:S(2)}) collective-permute-start(bf16[1,768,256]{2,1,0:T(8,128)(2,1)} %get-tuple-element.324), channel_id=1, source_target_pairs={{0,8},{4,12},{8,16},{12,20},{16,24},{20,28},{1,9},{5,13},{9,17},{1... | collective-permute-start | bytes 1179656 | tf_op jit(solution)/shard_map/ppermute | solution.py:349
  93.7 1.3 collective-permute-start.22
  95.0 2.5 %collective-permute-start.23 = (bf16[1,768,256]{2,1,0:T(8,128)(2,1)}, bf16[1,768,256]{2,1,0:T(8,128)(2,1)}, u32[]{:S(2)}, u32[]{:S(2)}) collective-permute-start(bf16[1,768,256]{2,1,0:T(8,128)(2,1)} %get-tuple-element.326), channel_id=1, source_target_pairs={{0,4},{4,0},{8,12},{12,8},{16,20},{20,16},{24,28},{28,24},{1,5},{5... | collective-permute-start | bytes 1179656 | tf_op jit(solution)/shard_map/ppermute | solution.py:351
  97.5 1.0 shard_map.131
  98.5 5.3 %collective-permute-start.27 = (bf16[1,768,256]{2,1,0:T(8,128)(2,1)}, bf16[1,768,256]{2,1,0:T(8,128)(2,1)}, u32[]{:S(2)}, u32[]{:S(2)}) collective-permute-start(bf16[1,768,256]{2,1,0:T(8,128)(2,1)} %get-tuple-element.335), channel_id=1, source_target_pairs={{0,8},{4,12},{8,16},{12,20},{16,24},{20,28},{1,9},{5,13},{9,17},{1... | collective-permute-start | bytes 1179656 | tf_op jit(solution)/shard_map/ppermute | solution.py:349
  103.8 1.3 collective-permute-start.28
  105.1 2.7 %collective-permute-start.29 = (bf16[1,768,256]{2,1,0:T(8,128)(2,1)}, bf16[1,768,256]{2,1,0:T(8,128)(2,1)}, u32[]{:S(2)}, u32[]{:S(2)}) collective-permute-start(bf16[1,768,256]{2,1,0:T(8,128)(2,1)} %get-tuple-element.337), channel_id=1, source_target_pairs={{0,4},{4,0},{8,12},{12,8},{16,20},{20,16},{24,28},{28,24},{1,5},{5... | collective-permute-start | bytes 1179656 | tf_op jit(solution)/shard_map/ppermute | solution.py:351
  107.8 1.0 shard_map.132
  108.8 2.8 %collective-permute-start.24 = (bf16[1,768,256]{2,1,0:T(8,128)(2,1)}, bf16[1,768,256]{2,1,0:T(8,128)(2,1)}, u32[]{:S(2)}, u32[]{:S(2)}) collective-permute-start(bf16[1,768,256]{2,1,0:T(8,128)(2,1)} %get-tuple-element.332), channel_id=1, source_target_pairs={{0,8},{4,12},{8,16},{12,20},{16,24},{20,28},{1,9},{5,13},{9,17},{1... | collective-permute-start | bytes 1179656 | tf_op jit(solution)/shard_map/ppermute | solution.py:349
  111.6 1.3 collective-permute-start.25
  112.9 2.4 %collective-permute-start.26 = (bf16[1,768,256]{2,1,0:T(8,128)(2,1)}, bf16[1,768,256]{2,1,0:T(8,128)(2,1)}, u32[]{:S(2)}, u32[]{:S(2)}) collective-permute-start(bf16[1,768,256]{2,1,0:T(8,128)(2,1)} %get-tuple-element.334), channel_id=1, source_target_pairs={{0,4},{4,0},{8,12},{12,8},{16,20},{20,16},{24,28},{28,24},{1,5},{5... | collective-permute-start | bytes 1179656 | tf_op jit(solution)/shard_map/ppermute | solution.py:351
  115.2 2.3 %add_convert_fusion = bf16[256,1024]{1,0:T(8,128)(2,1)} fusion(f32[256,1024]{1,0:T(8,128)} %get-tuple-element.294, bf16[256,1024]{1,0:T(8,128)(2,1)} %collective-permute-done.10), kind=kLoop, calls=%fused_computation | loop fusion | flops 786432 | bytes 2097152 | tf_op jit(solution)/shard_map/convert_element_type | solution.py:453
  117.5 4.7 %collective-permute-done.25 = bf16[1,768,256]{2,1,0:T(8,128)(2,1)} collective-permute-done((bf16[1,768,256]{2,1,0:T(8,128)(2,1)}, bf16[1,768,256]{2,1,0:T(8,128)(2,1)}, u32[]{:S(2)}, u32[]{:S(2)}) %collective-permute-start.25) | collective-permute-done | bytes 393248 | tf_op jit(solution)/shard_map/ppermute | solution.py:350
  122.2 0.1 collective-permute-done.26
  122.3 0.6 while.19
  122.9 6.2 %shard_map.134 = (bf16[4,2,768,256]{3,2,1,0:T(8,128)(2,1)}, bf16[4,2048]{1,0:T(4,128)(2,1)}) custom-call(s32[32]{0:T(128)S(1)} %get-tuple-element.548, s32[64]{0:T(128)} %refs_1_.1, s32[128]{0:T(128)S(1)} %get-tuple-element.338.refs_2_, bf16[4,2048]{1,0:T(4,128)(2,1)} %refs_3_.1, bf16[4,2,256]{2,1,0:T(2,128)(2,1)} %refs_4_.1, ...), custom_call_target="tpu_custom_call" | custom-call | flops 1000 | bytes 1000 | tf_op jit(solution)/shard_map/pallas_call | solution.py:413
  (28 shorter events, 0.1 us)
Async XLA Ops:
  0.6 32.2 %copy-start.2 = (s32[32]{0:T(128)S(1)}, s32[32]{0:T(128)}, u32[]{:S(2)}) copy-start(s32[32]{0:T(128)} %refs_0_.1) | copy-start | bytes 388
  4.7 28.1 %collective-permute-start.3 = (bf16[2,768,256]{2,1,0:T(8,128)(2,1)}, bf16[2,768,256]{2,1,0:T(8,128)(2,1)S(1)}, u32[]{:S(2)}, u32[]{:S(2)}) collective-permute-start(bf16[2,768,256]{2,1,0:T(8,128)(2,1)} %get-tuple-element.268), channel_id=1, source_target_pairs={{0,8},{4,12},{8,16},{12,20},{16,24},{20,28},{1,9},{5,13},{9,17},{1... | collective-permute-start | bytes 2359304 | tf_op jit(solution)/shard_map/ppermute | solution.py:349
  9.8 23.0 %collective-permute-start.4 = (bf16[2,768,256]{2,1,0:T(8,128)(2,1)}, bf16[2,768,256]{2,1,0:T(8,128)(2,1)S(1)}, u32[]{:S(2)}, u32[]{:S(2)}) collective-permute-start(bf16[2,768,256]{2,1,0:T(8,128)(2,1)} %get-tuple-element.269), channel_id=1, source_target_pairs={{8,0},{12,4},{16,8},{20,12},{24,16},{28,20},{9,1},{13,5},{17,9},{2... | collective-permute-start | bytes 2359304 | tf_op jit(solution)/shard_map/ppermute | solution.py:350
  11.1 21.7 %collective-permute-start.5 = (bf16[2,768,256]{2,1,0:T(8,128)(2,1)}, bf16[2,768,256]{2,1,0:T(8,128)(2,1)S(1)}, u32[]{:S(2)}, u32[]{:S(2)}) collective-permute-start(bf16[2,768,256]{2,1,0:T(8,128)(2,1)} %get-tuple-element.270), channel_id=1, source_target_pairs={{0,4},{4,0},{8,12},{12,8},{16,20},{20,16},{24,28},{28,24},{1,5},{5... | collective-permute-start | bytes 2359304 | tf_op jit(solution)/shard_map/ppermute | solution.py:351
  35.6 25.5 %collective-permute-start.9 = (f32[2,256,1024]{2,1,0:T(8,128)}, f32[2,256,1024]{2,1,0:T(8,128)}, u32[]{:S(2)}, u32[]{:S(2)}) collective-permute-start(f32[2,256,1024]{2,1,0:T(8,128)} %get-tuple-element.288), channel_id=1, source_target_pairs={{0,1},{1,0},{2,3},{3,2},{4,5},{5,4},{6,7},{7,6},{8,9},{9,8},{10,11... | collective-permute-start | bytes 6291464 | tf_op jit(solution)/shard_map/ppermute | solution.py:446
  35.7 14.4 %collective-permute-start.6 = (bf16[1,768,256]{2,1,0:T(8,128)(2,1)}, bf16[1,768,256]{2,1,0:T(8,128)(2,1)S(1)}, u32[]{:S(2)}, u32[]{:S(2)}) collective-permute-start(bf16[1,768,256]{2,1,0:T(8,128)(2,1)} %get-tuple-element.281), channel_id=1, source_target_pairs={{0,8},{4,12},{8,16},{12,20},{16,24},{20,28},{1,9},{5,13},{9,17},{1... | collective-permute-start | bytes 1179656 | tf_op jit(solution)/shard_map/ppermute | solution.py:349
  40.6 13.3 %collective-permute-start.7 = (bf16[1,768,256]{2,1,0:T(8,128)(2,1)}, bf16[1,768,256]{2,1,0:T(8,128)(2,1)S(1)}, u32[]{:S(2)}, u32[]{:S(2)}) collective-permute-start(bf16[1,768,256]{2,1,0:T(8,128)(2,1)} %get-tuple-element.282), channel_id=1, source_target_pairs={{8,0},{12,4},{16,8},{20,12},{24,16},{28,20},{9,1},{13,5},{17,9},{2... | collective-permute-start | bytes 1179656 | tf_op jit(solution)/shard_map/ppermute | solution.py:350
  41.9 12.4 %collective-permute-start.8 = (bf16[1,768,256]{2,1,0:T(8,128)(2,1)}, bf16[1,768,256]{2,1,0:T(8,128)(2,1)S(1)}, u32[]{:S(2)}, u32[]{:S(2)}) collective-permute-start(bf16[1,768,256]{2,1,0:T(8,128)(2,1)} %get-tuple-element.283), channel_id=1, source_target_pairs={{0,4},{4,0},{8,12},{12,8},{16,20},{20,16},{24,28},{28,24},{1,5},{5... | collective-permute-start | bytes 1179656 | tf_op jit(solution)/shard_map/ppermute | solution.py:351
  44.4 21.3 %collective-permute-start.11 = (bf16[1,768,256]{2,1,0:T(8,128)(2,1)}, bf16[1,768,256]{2,1,0:T(8,128)(2,1)}, u32[]{:S(2)}, u32[]{:S(2)}) collective-permute-start(bf16[1,768,256]{2,1,0:T(8,128)(2,1)} %get-tuple-element.299), channel_id=1, source_target_pairs={{0,8},{4,12},{8,16},{12,20},{16,24},{20,28},{1,9},{5,13},{9,17},{1... | collective-permute-start | bytes 1179656 | tf_op jit(solution)/shard_map/ppermute | solution.py:349
  50.1 15.6 %collective-permute-start.12 = (bf16[1,768,256]{2,1,0:T(8,128)(2,1)}, bf16[1,768,256]{2,1,0:T(8,128)(2,1)}, u32[]{:S(2)}, u32[]{:S(2)}) collective-permute-start(bf16[1,768,256]{2,1,0:T(8,128)(2,1)} %get-tuple-element.300), channel_id=1, source_target_pairs={{8,0},{12,4},{16,8},{20,12},{24,16},{28,20},{9,1},{13,5},{17,9},{2... | collective-permute-start | bytes 1179656 | tf_op jit(solution)/shard_map/ppermute | solution.py:350
  54.0 53.8 %copy-start = (bf16[1,768,256]{2,1,0:T(8,128)(2,1)}, bf16[1,768,256]{2,1,0:T(8,128)(2,1)S(1)}, u32[]{:S(2)}) copy-start(bf16[1,768,256]{2,1,0:T(8,128)(2,1)S(1)} %collective-permute-done.7.refs_4_.refs_10_) | copy-start | bytes 1179652
  54.0 11.8 %collective-permute-start.13 = (bf16[1,768,256]{2,1,0:T(8,128)(2,1)}, bf16[1,768,256]{2,1,0:T(8,128)(2,1)}, u32[]{:S(2)}, u32[]{:S(2)}) collective-permute-start(bf16[1,768,256]{2,1,0:T(8,128)(2,1)} %get-tuple-element.301), channel_id=1, source_target_pairs={{0,4},{4,0},{8,12},{12,8},{16,20},{20,16},{24,28},{28,24},{1,5},{5... | collective-permute-start | bytes 1179656 | tf_op jit(solution)/shard_map/ppermute | solution.py:351
  54.4 13.8 %copy-start.1 = (bf16[1,768,256]{2,1,0:T(8,128)(2,1)}, bf16[1,768,256]{2,1,0:T(8,128)(2,1)S(1)}, u32[]{:S(2)}) copy-start(bf16[1,768,256]{2,1,0:T(8,128)(2,1)S(1)} %collective-permute-done.8.refs_5_.refs_11_) | copy-start | bytes 1179652
  56.7 18.2 %collective-permute-start.14 = (bf16[1,768,256]{2,1,0:T(8,128)(2,1)}, bf16[1,768,256]{2,1,0:T(8,128)(2,1)}, u32[]{:S(2)}, u32[]{:S(2)}) collective-permute-start(bf16[1,768,256]{2,1,0:T(8,128)(2,1)} %get-tuple-element.305), channel_id=1, source_target_pairs={{0,8},{4,12},{8,16},{12,20},{16,24},{20,28},{1,9},{5,13},{9,17},{1... | collective-permute-start | bytes 1179656 | tf_op jit(solution)/shard_map/ppermute | solution.py:349
  61.1 13.9 %collective-permute-start.15 = (bf16[1,768,256]{2,1,0:T(8,128)(2,1)}, bf16[1,768,256]{2,1,0:T(8,128)(2,1)S(1)}, u32[]{:S(2)}, u32[]{:S(2)}) collective-permute-start(bf16[1,768,256]{2,1,0:T(8,128)(2,1)} %get-tuple-element.306), channel_id=1, source_target_pairs={{8,0},{12,4},{16,8},{20,12},{24,16},{28,20},{9,1},{13,5},{17,9},{2... | collective-permute-start | bytes 1179656 | tf_op jit(solution)/shard_map/ppermute | solution.py:350
  68.1 16.7 %collective-permute-start.16 = (bf16[1,768,256]{2,1,0:T(8,128)(2,1)}, bf16[1,768,256]{2,1,0:T(8,128)(2,1)}, u32[]{:S(2)}, u32[]{:S(2)}) collective-permute-start(bf16[1,768,256]{2,1,0:T(8,128)(2,1)} %get-tuple-element.311), channel_id=1, source_target_pairs={{0,8},{4,12},{8,16},{12,20},{16,24},{20,28},{1,9},{5,13},{9,17},{1... | collective-permute-start | bytes 1179656 | tf_op jit(solution)/shard_map/ppermute | solution.py:349
  73.7 12.8 %collective-permute-start.17 = (bf16[1,768,256]{2,1,0:T(8,128)(2,1)}, bf16[1,768,256]{2,1,0:T(8,128)(2,1)S(1)}, u32[]{:S(2)}, u32[]{:S(2)}) collective-permute-start(bf16[1,768,256]{2,1,0:T(8,128)(2,1)} %get-tuple-element.312), channel_id=1, source_target_pairs={{8,0},{12,4},{16,8},{20,12},{24,16},{28,20},{9,1},{13,5},{17,9},{2... | collective-permute-start | bytes 1179656 | tf_op jit(solution)/shard_map/ppermute | solution.py:350
  77.5 16.2 %collective-permute-start.18 = (bf16[1,768,256]{2,1,0:T(8,128)(2,1)}, bf16[1,768,256]{2,1,0:T(8,128)(2,1)}, u32[]{:S(2)}, u32[]{:S(2)}) collective-permute-start(bf16[1,768,256]{2,1,0:T(8,128)(2,1)} %get-tuple-element.317), channel_id=1, source_target_pairs={{0,8},{4,12},{8,16},{12,20},{16,24},{20,28},{1,9},{5,13},{9,17},{1... | collective-permute-start | bytes 1179656 | tf_op jit(solution)/shard_map/ppermute | solution.py:349
  83.5 11.5 %collective-permute-start.19 = (bf16[1,768,256]{2,1,0:T(8,128)(2,1)}, bf16[1,768,256]{2,1,0:T(8,128)(2,1)}, u32[]{:S(2)}, u32[]{:S(2)}) collective-permute-start(bf16[1,768,256]{2,1,0:T(8,128)(2,1)} %get-tuple-element.318), channel_id=1, source_target_pairs={{8,0},{12,4},{16,8},{20,12},{24,16},{28,20},{9,1},{13,5},{17,9},{2... | collective-permute-start | bytes 1179656 | tf_op jit(solution)/shard_map/ppermute | solution.py:350
  84.8 12.7 %collective-permute-start.20 = (bf16[1,768,256]{2,1,0:T(8,128)(2,1)}, bf16[1,768,256]{2,1,0:T(8,128)(2,1)}, u32[]{:S(2)}, u32[]{:S(2)}) collective-permute-start(bf16[1,768,256]{2,1,0:T(8,128)(2,1)} %get-tuple-element.319), channel_id=1, source_target_pairs={{0,4},{4,0},{8,12},{12,8},{16,20},{20,16},{24,28},{28,24},{1,5},{5... | collective-permute-start | bytes 1179656 | tf_op jit(solution)/shard_map/ppermute | solution.py:351
  84.9 26.7 %collective-permute-start.10 = (bf16[256,1024]{1,0:T(8,128)(2,1)}, bf16[256,1024]{1,0:T(8,128)(2,1)}, u32[]{:S(2)}, u32[]{:S(2)}) collective-permute-start(bf16[256,1024]{1,0:T(8,128)(2,1)} %get-tuple-element.295), channel_id=1, source_target_pairs={{0,2},{2,0},{1,3},{3,1},{4,6},{6,4},{5,7},{7,5},{8,10},{10,8},{9,1... | collective-permute-start | bytes 1572872 | tf_op jit(solution)/shard_map/ppermute | solution.py:451
  87.4 16.4 %collective-permute-start.21 = (bf16[1,768,256]{2,1,0:T(8,128)(2,1)}, bf16[1,768,256]{2,1,0:T(8,128)(2,1)}, u32[]{:S(2)}, u32[]{:S(2)}) collective-permute-start(bf16[1,768,256]{2,1,0:T(8,128)(2,1)} %get-tuple-element.324), channel_id=1, source_target_pairs={{0,8},{4,12},{8,16},{12,20},{16,24},{20,28},{1,9},{5,13},{9,17},{1... | collective-permute-start | bytes 1179656 | tf_op jit(solution)/shard_map/ppermute | solution.py:349
  93.7 11.4 %collective-permute-start.22 = (bf16[1,768,256]{2,1,0:T(8,128)(2,1)}, bf16[1,768,256]{2,1,0:T(8,128)(2,1)}, u32[]{:S(2)}, u32[]{:S(2)}) collective-permute-start(bf16[1,768,256]{2,1,0:T(8,128)(2,1)} %get-tuple-element.325), channel_id=1, source_target_pairs={{8,0},{12,4},{16,8},{20,12},{24,16},{28,20},{9,1},{13,5},{17,9},{2... | collective-permute-start | bytes 1179656 | tf_op jit(solution)/shard_map/ppermute | solution.py:350
  95.0 12.8 %collective-permute-start.23 = (bf16[1,768,256]{2,1,0:T(8,128)(2,1)}, bf16[1,768,256]{2,1,0:T(8,128)(2,1)}, u32[]{:S(2)}, u32[]{:S(2)}) collective-permute-start(bf16[1,768,256]{2,1,0:T(8,128)(2,1)} %get-tuple-element.326), channel_id=1, source_target_pairs={{0,4},{4,0},{8,12},{12,8},{16,20},{20,16},{24,28},{28,24},{1,5},{5... | collective-permute-start | bytes 1179656 | tf_op jit(solution)/shard_map/ppermute | solution.py:351
  98.5 14.3 %collective-permute-start.27 = (bf16[1,768,256]{2,1,0:T(8,128)(2,1)}, bf16[1,768,256]{2,1,0:T(8,128)(2,1)}, u32[]{:S(2)}, u32[]{:S(2)}) collective-permute-start(bf16[1,768,256]{2,1,0:T(8,128)(2,1)} %get-tuple-element.335), channel_id=1, source_target_pairs={{0,8},{4,12},{8,16},{12,20},{16,24},{20,28},{1,9},{5,13},{9,17},{1... | collective-permute-start | bytes 1179656 | tf_op jit(solution)/shard_map/ppermute | solution.py:349
  103.8 13.7 %collective-permute-start.28 = (bf16[1,768,256]{2,1,0:T(8,128)(2,1)}, bf16[1,768,256]{2,1,0:T(8,128)(2,1)}, u32[]{:S(2)}, u32[]{:S(2)}) collective-permute-start(bf16[1,768,256]{2,1,0:T(8,128)(2,1)} %get-tuple-element.336), channel_id=1, source_target_pairs={{8,0},{12,4},{16,8},{20,12},{24,16},{28,20},{9,1},{13,5},{17,9},{2... | collective-permute-start | bytes 1179656 | tf_op jit(solution)/shard_map/ppermute | solution.py:350
  105.1 12.4 %collective-permute-start.29 = (bf16[1,768,256]{2,1,0:T(8,128)(2,1)}, bf16[1,768,256]{2,1,0:T(8,128)(2,1)}, u32[]{:S(2)}, u32[]{:S(2)}) collective-permute-start(bf16[1,768,256]{2,1,0:T(8,128)(2,1)} %get-tuple-element.337), channel_id=1, source_target_pairs={{0,4},{4,0},{8,12},{12,8},{16,20},{20,16},{24,28},{28,24},{1,5},{5... | collective-permute-start | bytes 1179656 | tf_op jit(solution)/shard_map/ppermute | solution.py:351
  108.8 8.7 %collective-permute-start.24 = (bf16[1,768,256]{2,1,0:T(8,128)(2,1)}, bf16[1,768,256]{2,1,0:T(8,128)(2,1)}, u32[]{:S(2)}, u32[]{:S(2)}) collective-permute-start(bf16[1,768,256]{2,1,0:T(8,128)(2,1)} %get-tuple-element.332), channel_id=1, source_target_pairs={{0,8},{4,12},{8,16},{12,20},{16,24},{20,28},{1,9},{5,13},{9,17},{1... | collective-permute-start | bytes 1179656 | tf_op jit(solution)/shard_map/ppermute | solution.py:349
  111.6 10.7 %collective-permute-start.25 = (bf16[1,768,256]{2,1,0:T(8,128)(2,1)}, bf16[1,768,256]{2,1,0:T(8,128)(2,1)}, u32[]{:S(2)}, u32[]{:S(2)}) collective-permute-start(bf16[1,768,256]{2,1,0:T(8,128)(2,1)} %get-tuple-element.333), channel_id=1, source_target_pairs={{8,0},{12,4},{16,8},{20,12},{24,16},{28,20},{9,1},{13,5},{17,9},{2... | collective-permute-start | bytes 1179656 | tf_op jit(solution)/shard_map/ppermute | solution.py:350
  112.9 9.4 %collective-permute-start.26 = (bf16[1,768,256]{2,1,0:T(8,128)(2,1)}, bf16[1,768,256]{2,1,0:T(8,128)(2,1)}, u32[]{:S(2)}, u32[]{:S(2)}) collective-permute-start(bf16[1,768,256]{2,1,0:T(8,128)(2,1)} %get-tuple-element.334), channel_id=1, source_target_pairs={{0,4},{4,0},{8,12},{12,8},{16,20},{20,16},{24,28},{28,24},{1,5},{5... | collective-permute-start | bytes 1179656 | tf_op jit(solution)/shard_map/ppermute | solution.py:351
